TPU v7x, 512 devices: a whole 4x8x8 slice. The times are simulated.
512 devices in a mesh: row: 16 (over x, y_hi), col: 16 (over z, core), layer: 2 (over y_lo).
Axes of the slice: x: 4, y: 8 (y_hi: 4, y_lo: 2; y = y_hi * 2 + y_lo), z: 8, core: 2. Of those that a mesh axis runs over, the one named last changes fastest.
Arguments:
- a_blocks: bfloat16 [16, 16, 2, 16, 2, 128, 128], P('row', 'col', 'layer'), may hold values from -6 to 6
- a_cols: int32 [16, 16, 2, 16, 2], P('row', 'col', 'layer'), may hold values from 0 to 47, as said below
- a_count: int32 [16, 16, 2, 16], P('row', 'col', 'layer'), may hold values from 1 to 2
- b_blocks: bfloat16 [16, 16, 2, 48, 2, 128, 128], P('row', 'col', 'layer'), may hold values from -0.5 to 0.5
- b_cols: int32 [16, 16, 2, 48, 2], P('row', 'col', 'layer'), may hold values from 0 to 47, as said below
- b_count: int32 [16, 16, 2, 48], P('row', 'col', 'layer'), may hold values from 1 to 2
- c_cols: int32 [16, 16, 16, 2], P('row', 'col'), may hold values from 0 to 47, as said below
Outputs:
- c_blocks: bfloat16 [16, 16, 16, 2, 128, 128], P('row', 'col', 'layer')
Inputs may be any that keep to these rules, and one draw needn't show every extreme that they name: a_cols of block row r is one of 3 * r - 1, 3 * r, 3 * r + 1 modulo 48; the slots of one block row are distinct. b_cols of block row m is one of m - 1, m, m + 1 modulo 48; the slots of one block row are distinct. c_cols of block row r is one of 3 * r - 1, 3 * r, 3 * r + 1 modulo 48; the slots of one block row are distinct.
All inputs are finite; a program needn't handle non-finite values.
Results may differ from a plain program's by a relative error of at most 0.001.
Values may be sent and summed in bfloat16 or wider, within the bound.
No kernel may reach another device: no remote copies, remote signals or barrier semaphores. Data moves between devices by JAX's collectives and lax.ppermute only.
A program may use at most 64 MiB of HBM per device.

v0:
```python
import jax
import jax.numpy as jnp
from jax import lax
from jax.sharding import PartitionSpec as P

STEPS = 2


def passed_along(value, axis, steps):
    count = lax.axis_size(axis)
    pairs = [(source, (source + steps) % count) for source in range(count)]
    return lax.ppermute(value, axis, pairs)


def pick_rows(panel, index, live, wanted):
    return (
        jnp.take(panel, wanted, axis=0),
        jnp.take(index, wanted, axis=0),
        jnp.take(live, wanted, axis=0),
    )


def panel_terms(a_panel, a_live, chosen, chosen_cols, chosen_live, out_cols):
    slot_a = lax.broadcasted_iota(jnp.int32, chosen_cols.shape, 1)
    slot_b = lax.broadcasted_iota(jnp.int32, chosen_cols.shape, 2)
    usable = (slot_a < a_live[:, None, None]) & (slot_b < chosen_live[:, :, None])
    matches = (chosen_cols[:, :, :, None] == out_cols[:, None, None, :]) & usable[:, :, :, None]
    products = jnp.einsum("rtxy,rtuyz->rtuxz", a_panel, chosen, preferred_element_type=jnp.float32)
    return jnp.einsum(
        "rtuv,rtuxz->rvxz", matches.astype(jnp.float32), products, precision=lax.Precision.HIGHEST
    )


def local(a_blocks, a_cols, a_count, b_blocks, b_cols, b_count, c_cols):
    a_panel = a_blocks[0, 0, 0]
    a_index = a_cols[0, 0, 0]
    a_live = a_count[0, 0, 0]
    b_panel = b_blocks[0, 0, 0]
    b_index = b_cols[0, 0, 0]
    b_live = b_count[0, 0, 0]
    out_cols = c_cols[0, 0]
    partial_value = jnp.zeros(
        (out_cols.shape[0], out_cols.shape[1], a_panel.shape[2], b_panel.shape[3]), jnp.float32
    )
    for cannon_step in range(STEPS):
        if cannon_step > 0:
            a_panel, a_index, a_live = passed_along((a_panel, a_index, a_live), "col", -1)
        if cannon_step > 0:
            b_panel, b_index, b_live = passed_along((b_panel, b_index, b_live), "row", -1)
        chosen, chosen_cols, chosen_live = pick_rows(b_panel, b_index, b_live, a_index)
        partial_value = partial_value + panel_terms(
            a_panel, a_live, chosen, chosen_cols, chosen_live, out_cols
        )
    summed = lax.psum_scatter(partial_value, "layer", scatter_dimension=0, tiled=True)
    return summed.astype(jnp.bfloat16)[None, None]


def solution(mesh):
    return jax.shard_map(
        local,
        mesh=mesh,
        in_specs=(
            P("row", "col", "layer", None, None, None, None),
            P("row", "col", "layer", None, None),
            P("row", "col", "layer", None),
            P("row", "col", "layer", None, None, None, None),
            P("row", "col", "layer", None, None),
            P("row", "col", "layer", None),
            P("row", "col", None, None),
        ),
        out_specs=P("row", "col", "layer", None, None, None),
        check_vma=False,
    )
```

profile of v0, /device:TPU:1, one launch (start us, length us, event | category | flops | bytes accessed | tf_op | source)
XLA Modules:
  0.0 235.0 jit_solution(12557416722973179889)
XLA Ops:
  6.5 0.0 copy-start
  6.5 0.0 reduce-scatter.2.cloned.1.call-start
  6.5 9.0 %collective-permute-start.4 = (bf16[48,2,128,128]{3,2,1,0:T(8,128)(2,1)}, bf16[48,2,128,128]{3,2,1,0:T(8,128)(2,1)}, u32[]{:S(2)}, u32[]{:S(2)}) collective-permute-start(bf16[48,2,128,128]{3,2,1,0:T(8,128)(2,1)} %bitcast.54), channel_id=1, source_target_pairs={{0,480},{32,0},{64,32},{96,64},{128,96},{160,128},{192,160},{224,1... | collective-permute-start | bytes 9437192 | tf_op jit(solution)/shard_map/ppermute | solution.py:12
  15.6 1.0 collective-permute-start.2
  16.5 3.7 %collective-permute-start.3 = (s32[48]{0:T(128)}, s32[48]{0:T(128)S(1)}, u32[]{:S(2)}, u32[]{:S(2)}) collective-permute-start(s32[48]{0:T(128)} %bitcast.50), channel_id=1, source_target_pairs={{0,480},{32,0},{64,32},{96,64},{128,96},{160,128},{192,160},{224,1... | collective-permute-start | bytes 584 | tf_op jit(solution)/shard_map/ppermute | solution.py:12
  20.3 8.5 %collective-permute-start.1 = (s32[16,2]{0,1:T(2,128)}, s32[16,2]{0,1:T(2,128)S(1)}, u32[]{:S(2)}, u32[]{:S(2)}) collective-permute-start(s32[16,2]{0,1:T(2,128)} %bitcast.59), channel_id=1, source_target_pairs={{0,30},{2,0},{4,2},{6,4},{8,6},{10,8},{12,10},{14,12},{16,14},{18,... | collective-permute-start | bytes 392 | tf_op jit(solution)/shard_map/ppermute | solution.py:12
  28.8 0.7 collective-permute-start.5
  29.5 0.7 compare_select_fusion.1
  30.2 0.1 copy.53
  30.2 0.1 reshape.100
  30.3 0.0 copy-done
  30.4 0.7 gather_fusion.1
  31.0 0.0 copy-start.2
  31.1 0.0 copy-start.3
  31.1 0.0 copy-start.4
  31.1 2.9 %gather_fusion.2 = bf16[32,2,128,128]{3,2,1,0:T(8,128)(2,1)S(1)} fusion(bf16[48,2,128,128]{3,2,1,0:T(8,128)(2,1)} %bitcast.55, s32[1024]{0:T(1024)S(1)} %pad_clamp_fusion.1), kind=kCustom, calls=%fused_computation.2.clone | custom fusion | bytes 4194432 | tf_op jit(solution)/shard_map/jit(_take)/gather | solution.py:17
  34.0 0.1 reshape.107
  34.0 0.1 copy.59
  34.1 0.0 copy-done.2
  34.1 0.1 copy.52
  34.2 0.1 copy.60
  34.3 0.0 copy-done.3
  34.3 0.1 copy.57
  34.4 0.0 copy-done.4
  34.4 0.1 copy.54
  34.5 0.6 gather_fusion
  35.1 0.2 copy.84
  35.3 0.2 copy.56
  35.5 2.7 %copy.63 = bf16[16,2,2,128,128]{3,4,2,1,0:T(8,128)(2,1)} copy(bf16[16,2,2,128,128]{4,3,2,1,0:T(8,128)(2,1)S(1)} %bitcast.52) | data formatting | bytes 4194304 | tf_op jit(solution)/shard_map/jit(_take)/gather | solution.py:17
  38.2 0.0 copy-done.1
  38.2 4.3 %convolution_bitcast_fusion.1 = f32[16,2,2,128,128]{3,4,2,1,0:T(8,128)} fusion(bf16[16,2,2,128,128]{3,4,2,1,0:T(8,128)(2,1)} %copy.63, pred[16,2]{1,0:T(8,128)(4,1)S(1)} %copy.52, bf16[1,1,1,16,2,128,128]{6,5,4,3,2,1,0:T(8,128)(2,1)S(1)} %copy-done.1), kind=kOutput, calls=%fused_computation.7 | convolution fusion | flops 269484032 | bytes 7340064 | tf_op jit(solution)/shard_map/rtxy,rtuyz->rtuxz/dot_general | solution.py:28
  42.5 0.0 copy-start.5
  42.5 7.2 %copy.64 = f32[16,2,2,128,128]{4,2,1,3,0:T(2,128)} copy(f32[16,2,2,128,128]{3,4,2,1,0:T(8,128)} %convolution_bitcast_fusion.1) | data formatting | bytes 8388608 | tf_op jit(solution)/shard_map/rtxy,rtuyz->rtuxz/transpose | solution.py:28
  49.7 0.0 copy-done.5
  49.7 0.1 compare_and_fusion.1
  49.8 10.7 %fusion.9 = f32[16,2,128,128,1]{3,1,4,2,0:T(2,128)} fusion(f32[16,2,2,128,128]{4,2,1,3,0:T(2,128)} %copy.64, pred[16,2,2]{2,1,0:T(4,128)(4,1)S(1)} %compare_and_fusion.1, s32[16,2]{1,0:T(8,128)S(1)} %copy.57, s32[16,2,2]{2,1,0:T(2,128)S(1)} %copy.56), kind=kOutput, calls=%fused_computation.19 | convolution fusion | flops 25166080 | bytes 6291904 | tf_op jit(solution)/shard_map/rtuv,rtuxz->rvxz/dot_general | solution.py:29
  60.5 0.0 collective-permute-done.1
  60.5 2.1 collective-permute-start
  62.7 0.1 copy.67
  62.8 0.1 reshape.112
  62.9 88.1 %collective-permute-done.3 = s32[48]{0:T(128)S(1)} collective-permute-done((s32[48]{0:T(128)}, s32[48]{0:T(128)S(1)}, u32[]{:S(2)}, u32[]{:S(2)}) %collective-permute-start.3) | collective-permute-done | bytes 224 | tf_op jit(solution)/shard_map/ppermute | solution.py:12
  151.0 0.7 gather_fusion.4
  151.7 0.1 reshape.119
  151.8 0.1 copy.71
  151.9 0.1 copy.72
  152.0 0.0 collective-permute-done.2
  152.0 0.1 compare_and_fusion
  152.1 0.1 copy.65
  152.2 0.0 collective-permute-done
  152.2 0.6 gather_fusion.3
  152.8 0.2 copy.85
  153.0 0.2 copy.69
  153.2 0.0 collective-permute-done.4
  153.2 2.8 %gather_fusion.5 = bf16[32,2,128,128]{3,2,1,0:T(8,128)(2,1)S(1)} fusion(bf16[48,2,128,128]{3,2,1,0:T(8,128)(2,1)} %collective-permute-done.4, s32[1024]{0:T(1024)S(1)} %pad_clamp_fusion), kind=kCustom, calls=%fused_computation.5.clone | custom fusion | bytes 4194432 | tf_op jit(solution)/shard_map/jit(_take)/gather | solution.py:17
  156.1 2.7 %copy.75 = bf16[16,2,2,128,128]{3,4,2,1,0:T(8,128)(2,1)} copy(bf16[16,2,2,128,128]{4,3,2,1,0:T(8,128)(2,1)S(1)} %bitcast.53) | data formatting | bytes 4194304 | tf_op jit(solution)/shard_map/jit(_take)/gather | solution.py:17
  158.7 0.0 collective-permute-done.5
  158.7 4.6 %convolution_bitcast_fusion = f32[16,2,2,128,128]{3,4,2,1,0:T(8,128)} fusion(bf16[16,2,2,128,128]{3,4,2,1,0:T(8,128)(2,1)} %copy.75, pred[16,2]{1,0:T(8,128)(4,1)S(1)} %copy.65, bf16[16,2,128,128]{3,2,1,0:T(8,128)(2,1)} %collective-permute-done.5), kind=kOutput, calls=%fused_computation.6 | convolution fusion | flops 269484032 | bytes 7340064 | tf_op jit(solution)/shard_map/rtxy,rtuyz->rtuxz/dot_general | solution.py:28
  163.4 7.4 %copy.76 = f32[16,2,2,128,128]{4,2,1,3,0:T(2,128)} copy(f32[16,2,2,128,128]{3,4,2,1,0:T(8,128)} %convolution_bitcast_fusion) | data formatting | bytes 8388608 | tf_op jit(solution)/shard_map/rtxy,rtuyz->rtuxz/transpose | solution.py:28
  170.8 0.0 copy-done.6
  170.8 10.0 %bitcast_add_fusion = f32[16,2,128,128]{3,1,2,0:T(2,128)S(1)} fusion(f32[16,2,128,128,1]{3,1,4,2,0:T(2,128)S(1)} %copy-done.6, f32[16,2,2,128,128]{4,2,1,3,0:T(2,128)} %copy.76, pred[16,2,2]{2,1,0:T(4,128)(4,1)S(1)} %compare_and_fusion, s32[16,2,2]{2,1,0:T(2,128)S(1)} %copy.69, s32[16,2]{1,0:T(8,128)S(1)} %copy.57), kind=kOutput, calls=%fused_computation.8 | convolution fusion | flops 25690368 | bytes 8389056 | tf_op jit(solution)/shard_map/rtuv,rtuxz->rvxz/dot_general | solution.py:29
  180.8 1.6 copy.77
  182.4 0.0 reduce-scatter.2.cloned.1.call-update
  182.4 43.7 %reduce-scatter.2.cloned.1.call-done = f32[8,2,128,128]{3,2,1,0:T(8,128)} async-done(((f32[16,2,128,128]{3,2,1,0:T(8,128)}), f32[8,2,128,128]{3,2,1,0:T(8,128)}) %reduce-scatter.2.cloned.1.call-update) | async-done | bytes 1048592 | tf_op jit(solution)/shard_map/reduce_scatter | solution.py:54
  226.0 2.1 convert_bitcast_fusion
  (9 shorter events, 0.1 us)
Async XLA Ops:
  6.5 23.8 %copy-start = (s32[1,1,1,48]{3,2,1,0:T(1,128)S(1)}, s32[1,1,1,48]{3,2,1,0:T(1,128)}, u32[]{:S(2)}) copy-start(s32[1,1,1,48]{3,2,1,0:T(1,128)} %param.18) | copy-start | bytes 580
  6.5 219.5 %reduce-scatter.2.cloned.1.call-start = ((), (), s32[]{:S(2)}) async-start(), calls=%async_computation.1 | async-start | bytes 3145728 | tf_op jit(solution)/shard_map/reduce_scatter | solution.py:54
  6.5 146.7 %collective-permute-start.4 = (bf16[48,2,128,128]{3,2,1,0:T(8,128)(2,1)}, bf16[48,2,128,128]{3,2,1,0:T(8,128)(2,1)}, u32[]{:S(2)}, u32[]{:S(2)}) collective-permute-start(bf16[48,2,128,128]{3,2,1,0:T(8,128)(2,1)} %bitcast.54), channel_id=1, source_target_pairs={{0,480},{32,0},{64,32},{96,64},{128,96},{160,128},{192,160},{224,1... | collective-permute-start | bytes 9437192 | tf_op jit(solution)/shard_map/ppermute | solution.py:12
  15.6 136.4 %collective-permute-start.2 = (s32[16]{0:T(128)}, s32[16]{0:T(128)S(1)}, u32[]{:S(2)}, u32[]{:S(2)}) collective-permute-start(s32[16]{0:T(128)} %bitcast.62), channel_id=1, source_target_pairs={{0,30},{2,0},{4,2},{6,4},{8,6},{10,8},{12,10},{14,12},{16,14},{18,... | collective-permute-start | bytes 200 | tf_op jit(solution)/shard_map/ppermute | solution.py:12
  16.5 134.5 %collective-permute-start.3 = (s32[48]{0:T(128)}, s32[48]{0:T(128)S(1)}, u32[]{:S(2)}, u32[]{:S(2)}) collective-permute-start(s32[48]{0:T(128)} %bitcast.50), channel_id=1, source_target_pairs={{0,480},{32,0},{64,32},{96,64},{128,96},{160,128},{192,160},{224,1... | collective-permute-start | bytes 584 | tf_op jit(solution)/shard_map/ppermute | solution.py:12
  20.3 40.2 %collective-permute-start.1 = (s32[16,2]{0,1:T(2,128)}, s32[16,2]{0,1:T(2,128)S(1)}, u32[]{:S(2)}, u32[]{:S(2)}) collective-permute-start(s32[16,2]{0,1:T(2,128)} %bitcast.59), channel_id=1, source_target_pairs={{0,30},{2,0},{4,2},{6,4},{8,6},{10,8},{12,10},{14,12},{16,14},{18,... | collective-permute-start | bytes 392 | tf_op jit(solution)/shard_map/ppermute | solution.py:12
  28.8 129.9 %collective-permute-start.5 = (bf16[16,2,128,128]{3,2,1,0:T(8,128)(2,1)}, bf16[16,2,128,128]{3,2,1,0:T(8,128)(2,1)}, u32[]{:S(2)}, u32[]{:S(2)}) collective-permute-start(bf16[16,2,128,128]{3,2,1,0:T(8,128)(2,1)} %bitcast.56), channel_id=1, source_target_pairs={{0,30},{2,0},{4,2},{6,4},{8,6},{10,8},{12,10},{14,12},{16,14},{18,... | collective-permute-start | bytes 3145736 | tf_op jit(solution)/shard_map/ppermute | solution.py:12
  31.0 3.1 %copy-start.2 = (s32[1,1,1,16,2]{3,4,2,1,0:T(2,128)S(1)}, s32[1,1,1,16,2]{3,4,2,1,0:T(2,128)}, u32[]{:S(2)}) copy-start(s32[1,1,1,16,2]{3,4,2,1,0:T(2,128)} %param.14) | copy-start | bytes 388
  31.1 3.3 %copy-start.3 = (s32[1,1,16,2]{2,3,1,0:T(2,128)S(1)}, s32[1,1,16,2]{2,3,1,0:T(2,128)}, u32[]{:S(2)}) copy-start(s32[1,1,16,2]{2,3,1,0:T(2,128)} %param.19) | copy-start | bytes 388
  31.1 3.3 %copy-start.4 = (s32[1,1,1,48,2]{3,4,2,1,0:T(2,128)S(1)}, s32[1,1,1,48,2]{3,4,2,1,0:T(2,128)}, u32[]{:S(2)}) copy-start(s32[1,1,1,48,2]{3,4,2,1,0:T(2,128)} %param.17) | copy-start | bytes 1156
  35.5 2.7 %copy-start.1 = (bf16[1,1,1,16,2,128,128]{6,5,4,3,2,1,0:T(8,128)(2,1)S(1)}, bf16[1,1,1,16,2,128,128]{6,5,4,3,2,1,0:T(8,128)(2,1)}, u32[]{:S(2)}) copy-start(bf16[1,1,1,16,2,128,128]{6,5,4,3,2,1,0:T(8,128)(2,1)} %param.13) | copy-start | bytes 3145732
  42.5 7.2 %copy-start.5 = (s32[1,1,1,16]{3,2,1,0:T(1,128)S(1)}, s32[1,1,1,16]{3,2,1,0:T(1,128)}, u32[]{:S(2)}) copy-start(s32[1,1,1,16]{3,2,1,0:T(1,128)} %param.15) | copy-start | bytes 196
  60.5 91.7 %collective-permute-start = (s32[48,2]{1,0:T(8,128)S(1)}, s32[48,2]{1,0:T(8,128)S(1)}, u32[]{:S(2)}, u32[]{:S(2)}) collective-permute-start(s32[48,2]{1,0:T(8,128)S(1)} %copy.54), channel_id=1, source_target_pairs={{0,480},{32,0},{64,32},{96,64},{128,96},{160,128},{192,160},{224,1... | collective-permute-start | bytes 1160 | tf_op jit(solution)/shard_map/ppermute | solution.py:12
  163.4 7.4 %copy-start.6 = (f32[16,2,128,128,1]{3,1,4,2,0:T(2,128)S(1)}, f32[16,2,128,128,1]{3,1,4,2,0:T(2,128)}, u32[]{:S(2)}) copy-start(f32[16,2,128,128,1]{3,1,4,2,0:T(2,128)} %fusion.9) | copy-start | bytes 6291460
Sparse Core Ops, SparseCore 0:
  182.5 43.4 reduce-scatter.1
where the time goes:
time: 236 us; the launch traced here: 235 us
  waiting for transfers between devices  132 us (56%)
  local copies, waits for them, and re-layouts  31.9 us (14%)
  matrix products  29.6 us (13%)
  starting transfers between devices  25 us (11%)
  between operations  13.5 us (6%)
  other arithmetic  3.07 us (1%)
    ppermute x6, waiting for transfers between devices, passed_along(): return lax.ppermute(value, axis, pairs)  88.2 us
    reduce_scatter x1, waiting for transfers between devices, local(): lax.psum_scatter(partial_value, 'layer', scatter_dimension=0, tiled=True)  43.7 us
    ppermute x6, starting transfers between devices, passed_along(): return lax.ppermute(value, axis, pairs)  25 us
    dot_general x2, matrix products, panel_terms(): jnp.einsum('rtuv,rtuxz->rvxz', matches.astype(jnp.float32), products, pre...  20.7 us
    transpose x2, local copies, waits for them, and re-layouts, panel_terms(): jnp.einsum('rtxy,rtuyz->rtuxz', a_panel, chosen, preferred_element_type=j...  14.6 us
    gather x4, local copies, waits for them, and re-layouts, pick_rows(): jnp.take(panel, wanted, axis=0)  11.1 us
    dot_general x2, matrix products, panel_terms(): jnp.einsum('rtxy,rtuyz->rtuxz', a_panel, chosen, preferred_element_type=j...  8.97 us
  transfers between devices with their start and end apart: 7, of which 2 were waited for; matrix products, arithmetic and copies ran while one was open for 17% of the time, Pallas kernels for 0%

commit v1 on v0

v1 whole, which is shorter than its diff:
```python
import functools

import jax
import jax.numpy as jnp
from jax import lax
from jax.experimental import pallas as pl
from jax.experimental.pallas import tpu as pltpu
from jax.sharding import PartitionSpec as P

BS = 128
TOP = 32700.0
STEP = 0.08664339756999316
LEAST = 1e-33
TAIL = 16
VMEM_LIMIT = 40 * 1024 * 1024


def row_product(a_ref, a_row, b_ref, r, a_cols, a_count, b_cols, b_count, c_cols):
    slots_a, slots_b, slots_c = a_ref.shape[1], b_ref.shape[1], c_cols.shape[1]
    left, right = [], []
    for t in range(slots_a):
        m = a_cols[r, t]
        live = t < a_count[r]
        wide = []
        for v in range(slots_c):
            wanted = c_cols[r, v]
            slot = jnp.int32(0)
            found = jnp.int32(0)
            for u in range(slots_b):
                hit = live & (u < b_count[m]) & (b_cols[m, u] == wanted)
                slot = jnp.where(hit, jnp.int32(u), slot)
                found = jnp.where(hit, jnp.int32(1), found)
            block = b_ref[m, slot]
            wide.append(jnp.where(found == 1, block, jnp.zeros_like(block)))
        left.append(a_ref[a_row, t])
        right.append(jnp.concatenate(wide, axis=1))
    return jnp.dot(
        jnp.concatenate(left, axis=1),
        jnp.concatenate(right, axis=0),
        preferred_element_type=jnp.float32,
    )


def encode(value):
    peak = jnp.maximum(jnp.max(jnp.abs(value), axis=0, keepdims=True), LEAST)
    number = jnp.ceil(jnp.log(peak) * (1.0 / STEP))
    code = jnp.round(value * (TOP * jnp.exp(number * -STEP)))
    code = jnp.clip(code, -32767.0, 32767.0)
    return code.astype(jnp.int32).astype(jnp.int16), number.astype(jnp.int32)


def decode(code, number):
    scale = jnp.exp(number.astype(jnp.float32) * STEP) * (1.0 / TOP)
    return code.astype(jnp.int32).astype(jnp.float32) * scale


def store_payload(out_ref, products):
    numbers = []
    for k, value in enumerate(products):
        code, number = encode(value)
        out_ref[pl.ds(k * BS, BS), :] = code
        numbers.append(number)
    numbers += [jnp.zeros_like(numbers[0])] * (TAIL - len(numbers))
    tail = jnp.concatenate(numbers, axis=0)
    out_ref[pl.ds(len(products) * BS, TAIL), :] = tail.astype(jnp.int16)


def local_kernel(half, a_cols, a_count, b_cols, b_count, c_cols, a_ref, b_ref, own_ref, out_ref):
    rows = a_ref.shape[0] // 2
    lists = (a_cols, a_count, b_cols, b_count, c_cols)
    other = (1 - half[0]) * rows
    store_payload(
        out_ref, [row_product(a_ref, other + k, b_ref, other + k, *lists) for k in range(rows)]
    )
    own = half[0] * rows
    for k in range(rows):
        own_ref[pl.ds(k * BS, BS), :] = row_product(a_ref, own + k, b_ref, own + k, *lists)


def remote_kernel(first, a_cols, a_count, b_cols, b_count, c_cols, a_ref, b_ref, out_ref):
    lists = (a_cols, a_count, b_cols, b_count, c_cols)
    rows = a_ref.shape[0]
    store_payload(
        out_ref, [row_product(a_ref, k, b_ref, first[0] + k, *lists) for k in range(rows)]
    )


def add_payload(total, ref, k, rows):
    tail = ref[pl.ds(rows * BS, TAIL), :].astype(jnp.int32)
    return total + decode(ref[pl.ds(k * BS, BS), :], tail[k : k + 1, :])


def first_sum_kernel(own_ref, cross_ref, out_ref):
    rows = own_ref.shape[0] // BS
    for k in range(rows):
        out_ref[pl.ds(k * BS, BS), :] = add_payload(own_ref[pl.ds(k * BS, BS), :], cross_ref, k, rows)


def last_sum_kernel(half, sum_ref, layer_low, layer_high, same_ref, out_ref):
    rows, slots = out_ref.shape[0], out_ref.shape[1]

    def finish(layer_ref):
        for k in range(rows):
            total = add_payload(sum_ref[pl.ds(k * BS, BS), :], layer_ref, k, rows)
            total = add_payload(total, same_ref, k, rows)
            for v in range(slots):
                out_ref[k, v] = total[:, v * BS : (v + 1) * BS].astype(out_ref.dtype)

    @pl.when(half[0] == 0)
    def _():
        finish(layer_low)

    @pl.when(half[0] == 1)
    def _():
        finish(layer_high)


SMEM = pl.BlockSpec(memory_space=pltpu.SMEM)
VMEM = pl.BlockSpec(memory_space=pltpu.VMEM)


def call(kernel, scalars, arrays, outs, flops, moved, name):
    return pl.pallas_call(
        kernel,
        in_specs=[SMEM] * len(scalars) + [VMEM] * len(arrays),
        out_specs=jax.tree.map(lambda _: VMEM, outs),
        out_shape=outs,
        compiler_params=pltpu.CompilerParams(vmem_limit_bytes=VMEM_LIMIT),
        cost_estimate=pl.CostEstimate(flops=flops, bytes_accessed=moved, transcendentals=0),
        name=name,
    )(*scalars, *arrays)


def local(mesh_shape, a_blocks, a_cols, a_count, b_blocks, b_cols, b_count, c_cols):
    n_row, n_col = mesh_shape["row"], mesh_shape["col"]
    a_panel, b_panel = a_blocks[0, 0, 0], b_blocks[0, 0, 0]
    a_index, a_live = a_cols[0, 0, 0], a_count[0, 0, 0]
    b_index, b_live = b_cols[0, 0, 0], b_count[0, 0, 0]
    out_cols = c_cols[0, 0]
    layer = lax.axis_index("layer").astype(jnp.int32)
    rows = a_panel.shape[0] // 2
    wide = out_cols.shape[1] * BS
    coded = jax.ShapeDtypeStruct((rows * BS + TAIL, wide), jnp.int16)
    summed = jax.ShapeDtypeStruct((rows * BS, wide), jnp.float32)
    result = jax.ShapeDtypeStruct((rows, out_cols.shape[1], BS, BS), jnp.bfloat16)

    def place(i, j, l):
        return ((i % n_row) * n_col + j % n_col) * 2 + l

    grid = [(i, j, l) for i in range(n_row) for j in range(n_col) for l in range(2)]

    def send(value, target, who=(0, 1)):
        pairs = [(place(i, j, l), place(*target(i, j, l))) for i, j, l in grid if l in who]
        return lax.ppermute(value, ("row", "col", "layer"), pairs)

    def to_user(i, j, l):
        return i + 1, j - 1, l

    half = layer[None]
    own_first = (layer * rows)[None]
    other_first = ((1 - layer) * rows)[None]

    a_other = send(lax.dynamic_slice_in_dim(a_panel, other_first[0], rows, 0), to_user)
    far_lists = send(jnp.concatenate([a_index, a_live[:, None]], axis=1), to_user)
    far_cols = send(out_cols, lambda i, j, l: (i + 1, j, l))
    a_own = send(lax.dynamic_slice_in_dim(a_panel, own_first[0], rows, 0), to_user)

    block_flops = 2 * BS * 2 * BS * wide
    own, other = call(
        local_kernel,
        (half, a_index, a_live, b_index, b_live, out_cols),
        (a_panel, b_panel),
        (summed, coded),
        2 * rows * block_flops,
        6 << 20,
        "step0",
    )
    low = send(other, lambda i, j, l: (i, j, 0), who=(1,))

    far_index, far_live = far_lists[:, :-1], far_lists[:, -1]
    lists = (far_index, far_live, b_index, b_live, far_cols)
    cross = call(
        remote_kernel, (other_first, *lists), (a_other, b_panel), coded, rows * block_flops, 5 << 20, "step1_cross"
    )
    cross_in = send(cross, lambda i, j, l: (i - 1, j, 1 - l))

    a_own, cross = lax.optimization_barrier((a_own, cross))
    same = call(
        remote_kernel, (own_first, *lists), (a_own, b_panel), coded, rows * block_flops, 5 << 20, "step1_same"
    )
    same_in = send(same, lambda i, j, l: (i - 1, j, l))
    high = send(lax.optimization_barrier((other, a_own))[0], lambda i, j, l: (i, j, 1), who=(0,))

    total = call(first_sum_kernel, (), (own, cross_in), summed, 1 << 20, 3 << 20, "sum_cross")
    total, same_in = lax.optimization_barrier((total, same_in))
    c = call(
        last_sum_kernel, (half,), (total, low, high, same_in), result, 1 << 20, 3 << 20, "sum_all"
    )
    return c[None, None]


def solution(mesh):
    return jax.shard_map(
        functools.partial(local, dict(mesh.shape)),
        mesh=mesh,
        in_specs=(
            P("row", "col", "layer", None, None, None, None),
            P("row", "col", "layer", None, None),
            P("row", "col", "layer", None),
            P("row", "col", "layer", None, None, None, None),
            P("row", "col", "layer", None, None),
            P("row", "col", "layer", None),
            P("row", "col", None, None),
        ),
        out_specs=P("row", "col", "layer", None, None, None),
        check_vma=False,
    )
```

time: 236 us -> 113 us (0.48)
  waiting for transfers between devices: 132 us -> 60.7 us
  matrix products: 29.6 us -> 0 us
  local copies, waits for them, and re-layouts: 31.9 us -> 8.24 us
  between operations: 13.5 us -> 0.12 us
  starting transfers between devices: 25 us -> 35.8 us
  Pallas kernels: 0 us -> 6.76 us
  other arithmetic: 3.07 us -> 0.71 us
    reduce_scatter x1 -> x0, waiting for transfers between devices: 43.7 us -> none  [local(): lax.psum_scatter(partial_value, 'layer', scatter_dimension=0, tiled=True)]
    dot_general x4 -> x0, matrix products: 29.6 us -> none  [the longest x2 20.7 us: panel_terms(): jnp.einsum('rtuv,rtuxz->rvxz', matches.astype(jnp.float32), products, pre...]
    ppermute x6 -> x8, waiting for transfers between devices: 88.2 us -> 60.7 us  [send(): return lax.ppermute(value, ('row', 'col', 'layer'), pairs)]
    transpose x2 -> x0, local copies, waits for them, and re-layouts: 14.6 us -> none  [panel_terms(): jnp.einsum('rtxy,rtuyz->rtuxz', a_panel, chosen, preferred_element_type=j...]
    gather x14 -> x0, local copies, waits for them, and re-layouts: 14.4 us -> none  [the longest x4 11.1 us: pick_rows(): jnp.take(panel, wanted, axis=0)]
    ppermute x6 -> x8, starting transfers between devices: 25 us -> 35.8 us  [send(): return lax.ppermute(value, ('row', 'col', 'layer'), pairs)]
    pallas_call x0 -> x5, Pallas kernels: none -> 6.76 us  [call(): pl.pallas_call(kernel, in_specs=[SMEM] * len(scalars) + [VMEM] * len(arra...]
    unnamed x14 -> x10, local copies, waits for them, and re-layouts: 0.03 us -> 4.43 us
  transfers between devices with their start and end apart: 7 -> 8, of which waited for: 2 -> 4; matrix products, arithmetic and copies ran while one was open for 17% -> 3% of each run, Pallas kernels for 0% -> 5%
where the time goes in v1:
time: 113 us; the launch traced here: 112 us
  waiting for transfers between devices  60.7 us (54%)
  starting transfers between devices  35.8 us (32%)
  local copies, waits for them, and re-layouts  8.24 us (7%)
  Pallas kernels  6.76 us (6%)
    ppermute x8, waiting for transfers between devices, send(): return lax.ppermute(value, ('row', 'col', 'layer'), pairs)  60.7 us
    ppermute x8, starting transfers between devices, send(): return lax.ppermute(value, ('row', 'col', 'layer'), pairs)  35.8 us
    pallas_call x5, Pallas kernels, call(): pl.pallas_call(kernel, in_specs=[SMEM] * len(scalars) + [VMEM] * len(arra...  6.76 us
    unnamed x10, local copies, waits for them, and re-layouts  4.43 us
  transfers between devices with their start and end apart: 8, of which 4 were waited for; matrix products, arithmetic and copies ran while one was open for 3% of the time, Pallas kernels for 5%

profile of v1, /device:TPU:1, one launch (start us, length us, event | category | flops | bytes accessed | tf_op | source)
XLA Modules:
  0.0 112.3 jit_solution(7738465058815668056)
XLA Ops:
  0.0 1.3 %dynamic-slice_bitcast_fusion = (bf16[8,2,128,128]{3,2,1,0:T(8,128)(2,1)S(1)}, bf16[8,2,128,128]{3,2,1,0:T(8,128)(2,1)S(1)}) fusion(bf16[1,1,1,16,2,128,128]{6,5,4,3,2,1,0:T(8,128)(2,1)} %param.7, s32[]{:T(128)S(6)} %select_n.7, s32[]{:T(128)S(6)} %select_n.6), kind=kLoop, calls=%fused_computation | loop fusion | bytes 2097160 | tf_op jit(solution)/shard_map/dynamic_slice | solution.py:166
  1.3 5.6 %collective-permute-start.2 = (bf16[8,2,128,128]{3,2,1,0:T(8,128)(2,1)S(1)}, bf16[8,2,128,128]{3,2,1,0:T(8,128)(2,1)S(1)}, u32[]{:S(2)}, u32[]{:S(2)}) collective-permute-start(bf16[8,2,128,128]{3,2,1,0:T(8,128)(2,1)S(1)} %get-tuple-element.18), channel_id=1, source_target_pairs={{0,62},{1,63},{2,32},{3,33},{4,34},{5,35},{6,36},{7,37},{8,38},{9,... | collective-permute-start | bytes 1572872 | tf_op jit(solution)/shard_map/ppermute | solution.py:154
  6.9 13.6 %collective-permute-start.4 = (bf16[8,2,128,128]{3,2,1,0:T(8,128)(2,1)S(1)}, bf16[8,2,128,128]{3,2,1,0:T(8,128)(2,1)S(1)}, u32[]{:S(2)}, u32[]{:S(2)}) collective-permute-start(bf16[8,2,128,128]{3,2,1,0:T(8,128)(2,1)S(1)} %get-tuple-element.17), channel_id=1, source_target_pairs={{0,62},{1,63},{2,32},{3,33},{4,34},{5,35},{6,36},{7,37},{8,38},{9,... | collective-permute-start | bytes 1572872 | tf_op jit(solution)/shard_map/ppermute | solution.py:154
  20.5 0.8 copy.26.c_cols
  21.3 2.4 %collective-permute-start.1 = (s32[16,2]{1,0:T(8,128)S(1)}, s32[16,2]{1,0:T(8,128)S(1)}, u32[]{:S(2)}, u32[]{:S(2)}) collective-permute-start(s32[16,2]{1,0:T(8,128)S(1)} %copy.26.c_cols), channel_id=1, source_target_pairs={{0,32},{1,33},{2,34},{3,35},{4,36},{5,37},{6,38},{7,39},{8,40},{9,... | collective-permute-start | bytes 392 | tf_op jit(solution)/shard_map/ppermute | solution.py:154
  23.7 0.7 pad_add_fusion
  24.4 0.1 copy.27
  24.5 3.3 %collective-permute-start = (s32[16,3]{1,0:T(8,128)S(1)}, s32[16,3]{1,0:T(8,128)S(1)}, u32[]{:S(2)}, u32[]{:S(2)}) collective-permute-start(s32[16,3]{1,0:T(8,128)S(1)} %copy.27), channel_id=1, source_target_pairs={{0,62},{1,63},{2,32},{3,33},{4,34},{5,35},{6,36},{7,37},{8,38},{9,... | collective-permute-start | bytes 584 | tf_op jit(solution)/shard_map/ppermute | solution.py:154
  27.8 0.8 copy.24.a_cols
  28.5 0.8 copy.25.b_cols
  29.3 0.0 copy-start
  29.3 1.9 %copy-done = bf16[1,1,1,48,2,128,128]{6,5,4,3,2,1,0:T(8,128)(2,1)S(1)} copy-done((bf16[1,1,1,48,2,128,128]{6,5,4,3,2,1,0:T(8,128)(2,1)S(1)}, bf16[1,1,1,48,2,128,128]{6,5,4,3,2,1,0:T(8,128)(2,1)}, u32[]{:S(2)}) %copy-start) | copy-done | bytes 3145752
  31.2 0.0 copy-start.2
  31.2 1.2 %copy-done.2 = bf16[1,1,1,16,2,128,128]{6,5,4,3,2,1,0:T(8,128)(2,1)S(1)} copy-done((bf16[1,1,1,16,2,128,128]{6,5,4,3,2,1,0:T(8,128)(2,1)S(1)}, bf16[1,1,1,16,2,128,128]{6,5,4,3,2,1,0:T(8,128)(2,1)}, u32[]{:S(2)}) %copy-start.2) | copy-done | bytes 1048600
  32.4 0.0 copy-start.3
  32.4 0.7 copy-done.3
  33.1 0.0 copy-start.4
  33.1 0.7 copy-done.4
  33.7 0.0 copy-start.1
  33.7 2.0 %step0.1 = (f32[1024,256]{1,0:T(8,128)S(1)}, s16[1040,256]{1,0:T(8,128)(2,1)S(1)}) custom-call(s32[1]{0:T(128)} %bitcast.half, s32[16,2]{1,0:T(8,128)S(1)} %copy.24.a_cols, s32[16]{0:T(128)S(1)} %bitcast.27, s32[48,2]{1,0:T(8,128)S(1)} %copy.25.b_cols, s32[48]{0:T(128)S(1)} %bitcast.23, s32[16,2]{1,0:T(8,128)S(1)} %copy.26.c_cols, ...), custom_call_target="tpu_custom_call" | custom-call | flops 268435456 | bytes 6291456 | tf_op jit(solution)/shard_map/step0/pallas_call | solution.py:123
  35.7 1.3 %collective-permute-start.6 = (s16[1040,256]{1,0:T(8,128)(2,1)S(1)}, s16[1040,256]{1,0:T(8,128)(2,1)S(1)}, u32[]{:S(2)}, u32[]{:S(2)}) collective-permute-start(s16[1040,256]{1,0:T(8,128)(2,1)S(1)} %get-tuple-element.15), channel_id=1, source_target_pairs={{1,0},{3,2},{5,4},{7,6},{9,8},{11,10},{13,12},{15,14},{17,16},{19,... | collective-permute-start | bytes 1597448 | tf_op jit(solution)/shard_map/ppermute | solution.py:154
  37.0 13.7 %collective-permute-done = s32[16,3]{1,0:T(8,128)S(1)} collective-permute-done((s32[16,3]{1,0:T(8,128)S(1)}, s32[16,3]{1,0:T(8,128)S(1)}, u32[]{:S(2)}, u32[]{:S(2)}) %collective-permute-start) | collective-permute-done | bytes 224 | tf_op jit(solution)/shard_map/ppermute | solution.py:154
  50.7 0.2 slice_reduce_fusion.a_count
  50.9 9.6 %collective-permute-done.1.c_cols = s32[16,2]{1,0:T(8,128)S(1)} collective-permute-done((s32[16,2]{1,0:T(8,128)S(1)}, s32[16,2]{1,0:T(8,128)S(1)}, u32[]{:S(2)}, u32[]{:S(2)}) %collective-permute-start.1) | collective-permute-done | bytes 160 | tf_op jit(solution)/shard_map/ppermute | solution.py:154
  60.5 0.0 collective-permute-done.2.a_ref
  60.5 0.0 copy-done.1
  60.5 1.7 %step1_cross.1 = s16[1040,256]{1,0:T(8,128)(2,1)S(1)} custom-call(s32[1]{0:T(128)} %bitcast.8.first, s32[16,2]{1,0:T(8,128)S(1)} %bitcast.21, s32[16]{0:T(128)S(1)} %slice_reduce_fusion.a_count, s32[48,2]{1,0:T(8,128)S(1)} %copy.25.b_cols, s32[48]{0:T(128)S(1)} %bitcast.24, s32[16,2]{1,0:T(8,128)S(1)} %collective-permute-done.1.c_cols, ...), custom_call_target="tpu_custom_call" | custom-call | flops 134217728 | bytes 5242880 | tf_op jit(solution)/shard_map/step1_cross/pallas_call | solution.py:123
  62.3 2.0 %collective-permute-start.3 = (s16[1040,256]{1,0:T(8,128)(2,1)S(1)}, s16[1040,256]{1,0:T(8,128)(2,1)S(1)}, u32[]{:S(2)}, u32[]{:S(2)}) collective-permute-start(s16[1040,256]{1,0:T(8,128)(2,1)S(1)} %step1_cross.1), channel_id=1, source_target_pairs={{0,481},{1,480},{2,483},{3,482},{4,485},{5,484},{6,487},{7,486},{8... | collective-permute-start | bytes 1597448 | tf_op jit(solution)/shard_map/ppermute | solution.py:154
  64.3 0.0 collective-permute-done.4.a_ref
  64.3 1.7 %step1_same.1 = s16[1040,256]{1,0:T(8,128)(2,1)S(1)} custom-call(s32[1]{0:T(128)} %bitcast.11.first, s32[16,2]{1,0:T(8,128)S(1)} %bitcast.22, s32[16]{0:T(128)S(1)} %slice_reduce_fusion.a_count, s32[48,2]{1,0:T(8,128)S(1)} %copy.25.b_cols, s32[48]{0:T(128)S(1)} %bitcast.25, s32[16,2]{1,0:T(8,128)S(1)} %collective-permute-done.1.c_cols, ...), custom_call_target="tpu_custom_call" | custom-call | flops 134217728 | bytes 5242880 | tf_op jit(solution)/shard_map/step1_same/pallas_call | solution.py:123
  66.0 2.3 %collective-permute-start.5 = (s16[1040,256]{1,0:T(8,128)(2,1)S(1)}, s16[1040,256]{1,0:T(8,128)(2,1)S(1)}, u32[]{:S(2)}, u32[]{:S(2)}) collective-permute-start(s16[1040,256]{1,0:T(8,128)(2,1)S(1)} %step1_same.1), channel_id=1, source_target_pairs={{0,480},{1,481},{2,482},{3,483},{4,484},{5,485},{6,486},{7,487},{8... | collective-permute-start | bytes 1597448 | tf_op jit(solution)/shard_map/ppermute | solution.py:154
  68.3 5.3 %collective-permute-start.7 = (s16[1040,256]{1,0:T(8,128)(2,1)S(1)}, s16[1040,256]{1,0:T(8,128)(2,1)S(1)}, u32[]{:S(2)}, u32[]{:S(2)}) collective-permute-start(s16[1040,256]{1,0:T(8,128)(2,1)S(1)} %get-tuple-element.15), channel_id=1, source_target_pairs={{0,1},{2,3},{4,5},{6,7},{8,9},{10,11},{12,13},{14,15},{16,17},{18,... | collective-permute-start | bytes 1597448 | tf_op jit(solution)/shard_map/ppermute | solution.py:154
  73.6 11.2 %collective-permute-done.3.cross_ref = s16[1040,256]{1,0:T(8,128)(2,1)S(1)} collective-permute-done((s16[1040,256]{1,0:T(8,128)(2,1)S(1)}, s16[1040,256]{1,0:T(8,128)(2,1)S(1)}, u32[]{:S(2)}, u32[]{:S(2)}) %collective-permute-start.3) | collective-permute-done | bytes 532512 | tf_op jit(solution)/shard_map/ppermute | solution.py:154
  84.8 0.1 sum_cross.1.sum_ref
  85.0 26.2 %collective-permute-done.5.same_ref = s16[1040,256]{1,0:T(8,128)(2,1)S(1)} collective-permute-done((s16[1040,256]{1,0:T(8,128)(2,1)S(1)}, s16[1040,256]{1,0:T(8,128)(2,1)S(1)}, u32[]{:S(2)}, u32[]{:S(2)}) %collective-permute-start.5) | collective-permute-done | bytes 532512 | tf_op jit(solution)/shard_map/ppermute | solution.py:154
  111.2 0.0 collective-permute-done.6.layer_low
  111.2 0.0 collective-permute-done.7.layer_high
  111.2 1.1 %sum_all.1 = bf16[8,2,128,128]{3,2,1,0:T(8,128)(2,1)} custom-call(s32[1]{0:T(128)} %bitcast.half, f32[1024,256]{1,0:T(8,128)S(1)} %sum_cross.1.sum_ref, s16[1040,256]{1,0:T(8,128)(2,1)S(1)} %collective-permute-done.6.layer_low, s16[1040,256]{1,0:T(8,128)(2,1)S(1)} %collective-permute-done.7.layer_high, s16[1040,256]{1,0:T(8,128)(2,1)S(1)} %collective-permute-done.5.same_ref), custom_call_target="tpu_custom_call" | custom-call | flops 1048576 | bytes 3145728 | tf_op jit(solution)/shard_map/sum_all/pallas_call | solution.py:123
Async XLA Ops:
  1.3 59.2 %collective-permute-start.2 = (bf16[8,2,128,128]{3,2,1,0:T(8,128)(2,1)S(1)}, bf16[8,2,128,128]{3,2,1,0:T(8,128)(2,1)S(1)}, u32[]{:S(2)}, u32[]{:S(2)}) collective-permute-start(bf16[8,2,128,128]{3,2,1,0:T(8,128)(2,1)S(1)} %get-tuple-element.18), channel_id=1, source_target_pairs={{0,62},{1,63},{2,32},{3,33},{4,34},{5,35},{6,36},{7,37},{8,38},{9,... | collective-permute-start | bytes 1572872 | tf_op jit(solution)/shard_map/ppermute | solution.py:154
  6.9 57.4 %collective-permute-start.4 = (bf16[8,2,128,128]{3,2,1,0:T(8,128)(2,1)S(1)}, bf16[8,2,128,128]{3,2,1,0:T(8,128)(2,1)S(1)}, u32[]{:S(2)}, u32[]{:S(2)}) collective-permute-start(bf16[8,2,128,128]{3,2,1,0:T(8,128)(2,1)S(1)} %get-tuple-element.17), channel_id=1, source_target_pairs={{0,62},{1,63},{2,32},{3,33},{4,34},{5,35},{6,36},{7,37},{8,38},{9,... | collective-permute-start | bytes 1572872 | tf_op jit(solution)/shard_map/ppermute | solution.py:154
  21.3 39.2 %collective-permute-start.1 = (s32[16,2]{1,0:T(8,128)S(1)}, s32[16,2]{1,0:T(8,128)S(1)}, u32[]{:S(2)}, u32[]{:S(2)}) collective-permute-start(s32[16,2]{1,0:T(8,128)S(1)} %copy.26.c_cols), channel_id=1, source_target_pairs={{0,32},{1,33},{2,34},{3,35},{4,36},{5,37},{6,38},{7,39},{8,40},{9,... | collective-permute-start | bytes 392 | tf_op jit(solution)/shard_map/ppermute | solution.py:154
  24.5 26.2 %collective-permute-start = (s32[16,3]{1,0:T(8,128)S(1)}, s32[16,3]{1,0:T(8,128)S(1)}, u32[]{:S(2)}, u32[]{:S(2)}) collective-permute-start(s32[16,3]{1,0:T(8,128)S(1)} %copy.27), channel_id=1, source_target_pairs={{0,62},{1,63},{2,32},{3,33},{4,34},{5,35},{6,36},{7,37},{8,38},{9,... | collective-permute-start | bytes 584 | tf_op jit(solution)/shard_map/ppermute | solution.py:154
  29.3 1.9 %copy-start = (bf16[1,1,1,48,2,128,128]{6,5,4,3,2,1,0:T(8,128)(2,1)S(1)}, bf16[1,1,1,48,2,128,128]{6,5,4,3,2,1,0:T(8,128)(2,1)}, u32[]{:S(2)}) copy-start(bf16[1,1,1,48,2,128,128]{6,5,4,3,2,1,0:T(8,128)(2,1)} %param.10) | copy-start | bytes 9437188
  31.2 1.2 %copy-start.2 = (bf16[1,1,1,16,2,128,128]{6,5,4,3,2,1,0:T(8,128)(2,1)S(1)}, bf16[1,1,1,16,2,128,128]{6,5,4,3,2,1,0:T(8,128)(2,1)}, u32[]{:S(2)}) copy-start(bf16[1,1,1,16,2,128,128]{6,5,4,3,2,1,0:T(8,128)(2,1)} %param.7) | copy-start | bytes 3145732
  32.4 0.7 copy-start.3
  33.1 0.7 copy-start.4
  33.7 26.8 %copy-start.1 = (bf16[1,1,1,48,2,128,128]{6,5,4,3,2,1,0:T(8,128)(2,1)S(1)}, bf16[1,1,1,48,2,128,128]{6,5,4,3,2,1,0:T(8,128)(2,1)}, u32[]{:S(2)}) copy-start(bf16[1,1,1,48,2,128,128]{6,5,4,3,2,1,0:T(8,128)(2,1)} %param.10) | copy-start | bytes 9437188
  35.7 75.4 %collective-permute-start.6 = (s16[1040,256]{1,0:T(8,128)(2,1)S(1)}, s16[1040,256]{1,0:T(8,128)(2,1)S(1)}, u32[]{:S(2)}, u32[]{:S(2)}) collective-permute-start(s16[1040,256]{1,0:T(8,128)(2,1)S(1)} %get-tuple-element.15), channel_id=1, source_target_pairs={{1,0},{3,2},{5,4},{7,6},{9,8},{11,10},{13,12},{15,14},{17,16},{19,... | collective-permute-start | bytes 1597448 | tf_op jit(solution)/shard_map/ppermute | solution.py:154
  62.3 22.6 %collective-permute-start.3 = (s16[1040,256]{1,0:T(8,128)(2,1)S(1)}, s16[1040,256]{1,0:T(8,128)(2,1)S(1)}, u32[]{:S(2)}, u32[]{:S(2)}) collective-permute-start(s16[1040,256]{1,0:T(8,128)(2,1)S(1)} %step1_cross.1), channel_id=1, source_target_pairs={{0,481},{1,480},{2,483},{3,482},{4,485},{5,484},{6,487},{7,486},{8... | collective-permute-start | bytes 1597448 | tf_op jit(solution)/shard_map/ppermute | solution.py:154
  66.0 45.1 %collective-permute-start.5 = (s16[1040,256]{1,0:T(8,128)(2,1)S(1)}, s16[1040,256]{1,0:T(8,128)(2,1)S(1)}, u32[]{:S(2)}, u32[]{:S(2)}) collective-permute-start(s16[1040,256]{1,0:T(8,128)(2,1)S(1)} %step1_same.1), channel_id=1, source_target_pairs={{0,480},{1,481},{2,482},{3,483},{4,484},{5,485},{6,486},{7,487},{8... | collective-permute-start | bytes 1597448 | tf_op jit(solution)/shard_map/ppermute | solution.py:154
  68.3 42.8 %collective-permute-start.7 = (s16[1040,256]{1,0:T(8,128)(2,1)S(1)}, s16[1040,256]{1,0:T(8,128)(2,1)S(1)}, u32[]{:S(2)}, u32[]{:S(2)}) collective-permute-start(s16[1040,256]{1,0:T(8,128)(2,1)S(1)} %get-tuple-element.15), channel_id=1, source_target_pairs={{0,1},{2,3},{4,5},{6,7},{8,9},{10,11},{12,13},{14,15},{16,17},{18,... | collective-permute-start | bytes 1597448 | tf_op jit(solution)/shard_map/ppermute | solution.py:154

commit v2 on v1

v2 whole, which is shorter than its diff:
```python
import functools

import jax
import jax.numpy as jnp
from jax import lax
from jax.experimental import pallas as pl
from jax.experimental.pallas import tpu as pltpu
from jax.sharding import PartitionSpec as P

BS = 128
TOP = 32700.0
STEP = 0.08664339756999316
LEAST = 1e-33
TAIL = 16
SLOTS_A, SLOTS_C = 2, 2
B_COLS, B_COUNT, A_COLS, A_COUNT, C_COLS = 0, 2, 3, 5, 6
VMEM_LIMIT = 16 * 1024 * 1024


def row_product(a_ref, a_row, b_ref, r, a_lists, b_lists, c_lists):
    left, right = [], []
    for t in range(SLOTS_A):
        m = a_lists[A_COLS + t, r]
        live = t < a_lists[A_COUNT, r]
        wide = []
        for v in range(SLOTS_C):
            wanted = c_lists[C_COLS + v, r]
            slot = jnp.int32(0)
            found = jnp.int32(0)
            for u in range(b_ref.shape[1]):
                hit = live & (u < b_lists[B_COUNT, m]) & (b_lists[B_COLS + u, m] == wanted)
                slot = jnp.where(hit, jnp.int32(u), slot)
                found = jnp.where(hit, jnp.int32(1), found)
            block = b_ref[m, slot]
            wide.append(jnp.where(found == 1, block, jnp.zeros_like(block)))
        left.append(a_ref[pl.ds((a_row * SLOTS_A + t) * BS, BS), :])
        right.append(jnp.concatenate(wide, axis=1))
    return jnp.dot(
        jnp.concatenate(left, axis=1),
        jnp.concatenate(right, axis=0),
        preferred_element_type=jnp.float32,
    )


def pack_lists(b_cols, b_count, a_cols, a_count, c_cols):
    lists = [b_cols.T, b_count[None], a_cols.T, a_count[None], c_cols.T]
    depth, wide = sum(x.shape[0] for x in lists), b_count.shape[0]
    pack, at = 0, 0
    for x in lists:
        height = x.shape[0]
        pack += lax.pad(x, jnp.int32(0), [(at, depth - at - height, 0), (0, wide - x.shape[1], 0)])
        at += height
    return pack


def encode(value):
    peak = jnp.maximum(jnp.max(jnp.abs(value), axis=0, keepdims=True), LEAST)
    number = jnp.ceil(jnp.log(peak) * (1.0 / STEP))
    code = jnp.round(value * (TOP * jnp.exp(number * -STEP)))
    code = jnp.clip(code, -32767.0, 32767.0)
    return code.astype(jnp.int32).astype(jnp.int16), number.astype(jnp.int32)


def decode(code, number):
    scale = jnp.exp(number.astype(jnp.float32) * STEP) * (1.0 / TOP)
    return code.astype(jnp.int32).astype(jnp.float32) * scale


def store_payload(out_ref, products):
    numbers = []
    for k, value in enumerate(products):
        code, number = encode(value)
        out_ref[pl.ds(k * BS, BS), :] = code
        numbers.append(number)
    numbers += [jnp.zeros_like(numbers[0])] * (TAIL - len(numbers))
    tail = jnp.concatenate(numbers, axis=0)
    out_ref[pl.ds(len(products) * BS, TAIL), :] = tail.astype(jnp.int16)


def head_kernel(first, pack_ref, a_hbm, out_ref, tile, sem):
    size = out_ref.shape[0] - TAIL
    start = pl.multiple_of(first[0] * SLOTS_A * BS, BS)
    copy = pltpu.make_async_copy(a_hbm.at[pl.ds(start, size)], out_ref.at[pl.ds(0, size)], sem)
    copy.start()
    tile[...] = jnp.zeros_like(tile)
    tile[pl.ds(0, pack_ref.shape[0]), pl.ds(0, pack_ref.shape[1])] = pack_ref[...].astype(jnp.float32)
    out_ref[pl.ds(size, TAIL), :] = tile[...].astype(out_ref.dtype)
    copy.wait()


def local_kernel(parts, half, pack, a_ref, b_ref, low_ref, high_ref, out_ref, *sent):
    rows = a_ref.shape[0] // (2 * SLOTS_A * BS)
    other = (1 - half[0]) * rows
    own = half[0] * rows
    for (same, start, _), ref in zip(parts, sent, strict=True):
        at = pl.multiple_of((jnp.where(same, own, other) + start) * SLOTS_A * BS, BS)
        ref[...] = a_ref[pl.ds(at, ref.shape[0]), :]
    store_payload(
        out_ref, [row_product(a_ref, other + k, b_ref, other + k, pack, pack, pack) for k in range(rows)]
    )
    for k in range(rows):
        ref, at = (low_ref, k) if k < rows // 2 else (high_ref, k - rows // 2)
        ref[pl.ds(at * BS, BS), :] = row_product(a_ref, own + k, b_ref, own + k, pack, pack, pack)


def remote_kernel(first, a_lists, b_lists, c_lists, a_ref, b_ref, out_ref):
    rows = a_ref.shape[0] // (SLOTS_A * BS)
    store_payload(
        out_ref,
        [row_product(a_ref, k, b_ref, first[0] + k, a_lists, b_lists, c_lists) for k in range(rows)],
    )


def payload_row(ref, k):
    rows = (ref.shape[0] - TAIL) // BS
    tail = ref[pl.ds(rows * BS, TAIL), :].astype(jnp.int32)
    return decode(ref[pl.ds(k * BS, BS), :], tail[k : k + 1, :])


def add_kernel(start, wanted, half, total_ref, layer_ref, part_ref, out_ref):
    rows = out_ref.shape[0] // BS
    for k in range(rows):
        out_ref[pl.ds(k * BS, BS), :] = total_ref[pl.ds(k * BS, BS), :] + payload_row(part_ref, k)

    @pl.when(half[0] == wanted)
    def _():
        for k in range(rows):
            out_ref[pl.ds(k * BS, BS), :] += payload_row(layer_ref, start + k)


def third_sum_kernel(half, low_ref, high_ref, layer_ref, part_ref, out_ref, rest_ref):
    rows = low_ref.shape[0] // BS
    slots = out_ref.shape[1]
    scale = jnp.where(half[0] == 1, 1.0, 0.0)
    for k in range(rows):
        total = low_ref[pl.ds(k * BS, BS), :] + payload_row(part_ref, k)
        total = total + jnp.where(half[0] == 1, payload_row(layer_ref, k), 0.0)
        for v in range(slots):
            out_ref[k, v] = total[:, v * BS : (v + 1) * BS].astype(out_ref.dtype)
        rest = jnp.where(half[0] == 1, payload_row(layer_ref, rows + k), 0.0)
        rest_ref[pl.ds(k * BS, BS), :] = high_ref[pl.ds(k * BS, BS), :] + rest


def last_sum_kernel(rest_ref, part_ref, _, out_ref):
    for k in range(out_ref.shape[0]):
        total = rest_ref[pl.ds(k * BS, BS), :] + payload_row(part_ref, k)
        for v in range(out_ref.shape[1]):
            out_ref[k, v] = total[:, v * BS : (v + 1) * BS].astype(out_ref.dtype)


SMEM = pl.BlockSpec(memory_space=pltpu.SMEM)
VMEM = pl.BlockSpec(memory_space=pltpu.VMEM)
HBM = pl.BlockSpec(memory_space=pltpu.HBM)


def call(kernel, scalars, arrays, outs, cost, name, out_specs=None, **more):
    return pl.pallas_call(
        kernel,
        in_specs=[SMEM] * len(scalars) + [VMEM] * len(arrays),
        out_specs=jax.tree.map(lambda _: VMEM, outs) if out_specs is None else out_specs,
        out_shape=outs,
        compiler_params=pltpu.CompilerParams(vmem_limit_bytes=VMEM_LIMIT),
        cost_estimate=pl.CostEstimate(flops=int(cost * US), bytes_accessed=0, transcendentals=0),
        name=name,
        **more,
    )(*scalars, *arrays)


PARTS = ((False, 0, 4), (False, 4, 4), (True, 0, 4), (True, 4, 4))
US = 1e9
COST_STEP0 = 2
COST_STEP1 = 10
COST_SUM = 10


def after(value, *others):
    return lax.optimization_barrier((value, *others))[0]


def local(mesh_shape, a_blocks, a_cols, a_count, b_blocks, b_cols, b_count, c_cols):
    n_row, n_col = mesh_shape["row"], mesh_shape["col"]
    a_panel, b_panel = a_blocks[0, 0, 0], b_blocks[0, 0, 0]
    a_index, a_live = a_cols[0, 0, 0], a_count[0, 0, 0]
    b_index, b_live = b_cols[0, 0, 0], b_count[0, 0, 0]
    out_cols = c_cols[0, 0]
    layer = lax.axis_index("layer").astype(jnp.int32)
    rows = a_panel.shape[0] // 2
    wide = out_cols.shape[1] * BS
    summed = jax.ShapeDtypeStruct((rows // 2 * BS, wide), jnp.float32)
    result = jax.ShapeDtypeStruct((rows, out_cols.shape[1], BS, BS), jnp.bfloat16)

    def coded(count):
        return jax.ShapeDtypeStruct((count * BS + TAIL, wide), jnp.int16)

    def place(i, j, l):
        return ((i % n_row) * n_col + j % n_col) * 2 + l

    grid = [(i, j, l) for i in range(n_row) for j in range(n_col) for l in range(2)]

    def send(name, value, target, who=(0, 1)):
        pairs = [(place(i, j, l), place(*target(i, j, l))) for i, j, l in grid if l in who]
        with jax.named_scope(name):
            return lax.ppermute(value, ("row", "col", "layer"), pairs)

    def to_user(i, j, l):
        return i + 1, j - 1, l

    half = layer[None]
    firsts = [jnp.where(same, layer, 1 - layer) * rows + start for same, start, _ in PARTS]

    pack = pack_lists(b_index, b_live, a_index, a_live, out_cols)
    row_size = SLOTS_A * BS
    a_panel = a_panel.reshape(-1, BS)
    head = pl.pallas_call(
        head_kernel,
        in_specs=[SMEM, VMEM, HBM],
        out_specs=VMEM,
        out_shape=jax.ShapeDtypeStruct((PARTS[0][2] * row_size + TAIL, BS), a_panel.dtype),
        scratch_shapes=[pltpu.VMEM((TAIL, BS), jnp.float32), pltpu.SemaphoreType.DMA],
        compiler_params=pltpu.CompilerParams(vmem_limit_bytes=VMEM_LIMIT),
        name="head",
    )(firsts[0][None], pack, a_panel)
    far_a = [send("send_a0", head, to_user)]

    parts = PARTS[1:]
    low, high, other, *a_parts = call(
        functools.partial(local_kernel, parts),
        (half, pack),
        (a_panel, b_panel),
        (
            summed,
            summed,
            coded(rows),
            *(jax.ShapeDtypeStruct((count * row_size, BS), a_panel.dtype) for _, _, count in parts),
        ),
        COST_STEP0,
        "step0",
    )
    down = send("send_layer_down", other, lambda i, j, l: (i, j, 0), who=(1,))
    far_cols = send("send_c_cols", after(pack, other), lambda i, j, l: (i + 1, j, l))
    far_a += [send(f"send_a{k + 1}", after(part, far_cols), to_user) for k, part in enumerate(a_parts[:-1])]

    far_lists = far_a[0][-TAIL:, : pack.shape[1]].astype(jnp.int32)
    back, before = [], []
    for k, ((same, _, count), first) in enumerate(zip(PARTS, firsts, strict=True)):
        product = call(
            remote_kernel,
            (first[None], far_lists, pack, far_cols),
            (after(far_a[k], *before), b_panel),
            coded(count),
            COST_STEP1,
            f"step1_part{k}",
        )
        before = [product]
        if k == 0:
            before.append(down)
            far_a.append(send(f"send_a{len(far_a)}", after(a_parts[-1], product), to_user))
        back.append(send(f"send_c{k}", product, lambda i, j, l, same=same: (i - 1, j, l if same else 1 - l)))
    up = send("send_layer_up", after(other, product), lambda i, j, l: (i, j, 1), who=(0,))

    add = functools.partial(call, outs=summed, cost=COST_SUM)
    low = add(functools.partial(add_kernel, 0, 0), (half,), (low, down, back[0]), name="sum_part0")
    high = add(functools.partial(add_kernel, rows // 2, 0), (half,), (after(high, low), down, back[1]), name="sum_part1")
    c, rest = call(third_sum_kernel, (half,), (low, high, up, back[2]), (result, summed), COST_SUM, "sum_part2")
    c = pl.pallas_call(
        last_sum_kernel,
        grid=(1,),
        in_specs=[pl.BlockSpec(summed.shape, lambda _: (0, 0)), pl.BlockSpec(coded(rows // 2).shape, lambda _: (0, 0)), pl.BlockSpec(memory_space=pl.ANY)],
        out_specs=pl.BlockSpec((rows // 2, *result.shape[1:]), lambda _: (1, 0, 0, 0)),
        out_shape=result,
        input_output_aliases={2: 0},
        compiler_params=pltpu.CompilerParams(vmem_limit_bytes=VMEM_LIMIT),
        name="sum_part3",
    )(rest, back[3], c)
    return c[None, None]


def solution(mesh):
    return jax.shard_map(
        functools.partial(local, dict(mesh.shape)),
        mesh=mesh,
        in_specs=(
            P("row", "col", "layer", None, None, None, None),
            P("row", "col", "layer", None, None),
            P("row", "col", "layer", None),
            P("row", "col", "layer", None, None, None, None),
            P("row", "col", "layer", None, None),
            P("row", "col", "layer", None),
            P("row", "col", None, None),
        ),
        out_specs=P("row", "col", "layer", None, None, None),
        check_vma=False,
    )
```

time: 113 us -> 96 us (0.85)
  the two profiles are of different devices: /device:TPU:1 before, /device:TPU:54 now
where the time goes in v2:
time: 96 us; the launch traced here: 95.5 us
  starting transfers between devices  45.2 us (47%)
  waiting for transfers between devices  34.7 us (36%)
  Pallas kernels  8.36 us (9%)
  local copies, waits for them, and re-layouts  6.21 us (6%)
    ppermute x11, starting transfers between devices, send(): return lax.ppermute(value, ('row', 'col', 'layer'), pairs)  45.2 us
    ppermute x11, waiting for transfers between devices, send(): return lax.ppermute(value, ('row', 'col', 'layer'), pairs)  34.7 us
    pallas_call x8, Pallas kernels, call(): pl.pallas_call(kernel, in_specs=[SMEM] * len(scalars) + [VMEM] * len(arra...  7.54 us
    unnamed x8, local copies, waits for them, and re-layouts  6.21 us
  transfers between devices with their start and end apart: 11, of which 6 were waited for; matrix products, arithmetic and copies ran while one was open for 0% of the time, Pallas kernels for 8%

profile of v2, /device:TPU:54, one launch (start us, length us, event | category | flops | bytes accessed | tf_op | source)
XLA Modules:
  0.0 95.5 jit_solution(1659277935013811277)
XLA Ops:
  0.0 0.8 pad_add_fusion.pack.pack_ref.b_lists
  0.8 0.0 copy-start
  0.8 1.2 %copy-done = bf16[1,1,1,16,2,128,128]{6,5,4,3,2,1,0:T(8,128)(2,1)S(1)} copy-done((bf16[1,1,1,16,2,128,128]{6,5,4,3,2,1,0:T(8,128)(2,1)S(1)}, bf16[1,1,1,16,2,128,128]{6,5,4,3,2,1,0:T(8,128)(2,1)}, u32[]{:S(2)}) %copy-start) | copy-done | bytes 1048600
  2.0 9.6 %collective-permute-start.1 = (bf16[1040,128]{1,0:T(8,128)(2,1)S(1)}, bf16[1040,128]{1,0:T(8,128)(2,1)S(1)}, u32[]{:S(2)}, u32[]{:S(2)}) collective-permute-start(bf16[1040,128]{1,0:T(8,128)(2,1)S(1)} %head.1), channel_id=1, source_target_pairs={{0,62},{1,63},{2,32},{3,33},{4,34},{5,35},{6,36},{7,37},{8,38},{9,... | collective-permute-start | bytes 798728 | tf_op jit(solution)/shard_map/send_a0/ppermute | solution.py:203
  11.7 0.0 copy-start.1
  11.7 1.2 %copy-done.1 = bf16[1,1,1,16,2,128,128]{6,5,4,3,2,1,0:T(8,128)(2,1)S(1)} copy-done((bf16[1,1,1,16,2,128,128]{6,5,4,3,2,1,0:T(8,128)(2,1)S(1)}, bf16[1,1,1,16,2,128,128]{6,5,4,3,2,1,0:T(8,128)(2,1)}, u32[]{:S(2)}) %copy-start.1) | copy-done | bytes 1048600
  12.9 0.0 copy-start.2
  12.9 1.9 %copy-done.2 = bf16[1,1,1,48,2,128,128]{6,5,4,3,2,1,0:T(8,128)(2,1)S(1)} copy-done((bf16[1,1,1,48,2,128,128]{6,5,4,3,2,1,0:T(8,128)(2,1)S(1)}, bf16[1,1,1,48,2,128,128]{6,5,4,3,2,1,0:T(8,128)(2,1)}, u32[]{:S(2)}) %copy-start.2) | copy-done | bytes 3145752
  14.8 1.5 %step0.1 = (f32[512,256]{1,0:T(8,128)S(1)}, f32[512,256]{1,0:T(8,128)S(1)}, s16[1040,256]{1,0:T(8,128)(2,1)S(1)}, bf16[1024,128]{1,0:T(8,128)(2,1)S(1)}, bf16[10...) custom-call(s32[1]{0:T(128)} %bitcast.half, s32[8,48]{1,0:T(8,128)S(1)} %pad_add_fusion.pack.pack_ref.b_lists, ...), custom_call_target="tpu_custom_call" | custom-call | flops 2000000000 | tf_op jit(solution)/shard_map/step0/pallas_call | solution.py:157
  16.3 4.5 %collective-permute-start.2 = (s32[8,48]{1,0:T(8,128)S(1)}, s32[8,48]{1,0:T(8,128)S(1)}, u32[]{:S(2)}, u32[]{:S(2)}) collective-permute-start(s32[8,48]{1,0:T(8,128)S(1)} %pad_add_fusion.pack.pack_ref.b_lists), channel_id=1, source_target_pairs={{0,32},{1,33},{2,34},{3,35},{4,36},{5,37},{6,38},{7,39},{8,40},{9,... | collective-permute-start | bytes 4616 | tf_op jit(solution)/shard_map/send_c_cols/ppermute | solution.py:203
  20.8 1.3 %collective-permute-start = (s16[1040,256]{1,0:T(8,128)(2,1)S(1)}, s16[1040,256]{1,0:T(8,128)(2,1)S(1)}, u32[]{:S(2)}, u32[]{:S(2)}) collective-permute-start(s16[1040,256]{1,0:T(8,128)(2,1)S(1)} %get-tuple-element.36), channel_id=1, source_target_pairs={{1,0},{3,2},{5,4},{7,6},{9,8},{11,10},{13,12},{15,14},{17,16},{19,... | collective-permute-start | bytes 1597448 | tf_op jit(solution)/shard_map/send_layer_down/ppermute | solution.py:203
  22.1 0.8 collective-permute-done.2.c_lists
  22.9 6.7 %collective-permute-start.4 = (bf16[1024,128]{1,0:T(8,128)(2,1)S(1)}, bf16[1024,128]{1,0:T(8,128)(2,1)S(1)}, u32[]{:S(2)}, u32[]{:S(2)}) collective-permute-start(bf16[1024,128]{1,0:T(8,128)(2,1)S(1)} %get-tuple-element.28), channel_id=1, source_target_pairs={{0,62},{1,63},{2,32},{3,33},{4,34},{5,35},{6,36},{7,37},{8,38},{9,... | collective-permute-start | bytes 786440 | tf_op jit(solution)/shard_map/send_a1/ppermute | solution.py:203
  29.7 4.5 %collective-permute-start.7 = (bf16[1024,128]{1,0:T(8,128)(2,1)S(1)}, bf16[1024,128]{1,0:T(8,128)(2,1)S(1)}, u32[]{:S(2)}, u32[]{:S(2)}) collective-permute-start(bf16[1024,128]{1,0:T(8,128)(2,1)S(1)} %get-tuple-element.33), channel_id=1, source_target_pairs={{0,62},{1,63},{2,32},{3,33},{4,34},{5,35},{6,36},{7,37},{8,38},{9,... | collective-permute-start | bytes 786440 | tf_op jit(solution)/shard_map/send_a2/ppermute | solution.py:203
  34.2 0.0 collective-permute-done.1.a_ref
  34.2 0.0 copy-start.3
  34.2 1.9 %copy-done.3 = bf16[1,1,1,48,2,128,128]{6,5,4,3,2,1,0:T(8,128)(2,1)S(1)} copy-done((bf16[1,1,1,48,2,128,128]{6,5,4,3,2,1,0:T(8,128)(2,1)S(1)}, bf16[1,1,1,48,2,128,128]{6,5,4,3,2,1,0:T(8,128)(2,1)}, u32[]{:S(2)}) %copy-start.3) | copy-done | bytes 3145752
  36.1 1.2 %step1_part0.1 = s16[528,256]{1,0:T(8,128)(2,1)S(1)} custom-call(s32[1]{0:T(128)} %bitcast.11.first, s32[16,48]{1,0:T(8,128)S(1)} %slice_convert_fusion.a_lists, s32[8,48]{1,0:T(8,128)S(1)} %pad_add_fusion.pack.pack_ref.b_lists, s32[8,48]{1,0:T(8,128)S(1)} %collective-permute-done.2.c_lists, bf16[1040,128]{1,0:T(8,128)(2,1)S(1)} %collective-permute-done.1.a_ref, ...), custom_call_target="tpu_custom_call" | custom-call | flops 10000000000 | tf_op jit(solution)/shard_map/step1_part0/pallas_call | solution.py:157
  37.3 5.3 %collective-permute-start.3 = (s16[528,256]{1,0:T(8,128)(2,1)S(1)}, s16[528,256]{1,0:T(8,128)(2,1)S(1)}, u32[]{:S(2)}, u32[]{:S(2)}) collective-permute-start(s16[528,256]{1,0:T(8,128)(2,1)S(1)} %step1_part0.1), channel_id=1, source_target_pairs={{0,481},{1,480},{2,483},{3,482},{4,485},{5,484},{6,487},{7,486},{8... | collective-permute-start | bytes 811016 | tf_op jit(solution)/shard_map/send_c0/ppermute | solution.py:203
  42.5 5.0 %collective-permute-start.6 = (bf16[1024,128]{1,0:T(8,128)(2,1)S(1)}, bf16[1024,128]{1,0:T(8,128)(2,1)S(1)}, u32[]{:S(2)}, u32[]{:S(2)}) collective-permute-start(bf16[1024,128]{1,0:T(8,128)(2,1)S(1)} %get-tuple-element.31), channel_id=1, source_target_pairs={{0,62},{1,63},{2,32},{3,33},{4,34},{5,35},{6,36},{7,37},{8,38},{9,... | collective-permute-start | bytes 786440 | tf_op jit(solution)/shard_map/send_a3/ppermute | solution.py:203
  47.5 0.0 collective-permute-done.4.a_ref
  47.5 0.0 collective-permute-done.layer_ref
  47.5 1.2 %step1_part1.1 = s16[528,256]{1,0:T(8,128)(2,1)S(1)} custom-call(s32[1]{0:T(128)} %bitcast.12.first, s32[16,48]{1,0:T(8,128)S(1)} %slice_convert_fusion.a_lists, s32[8,48]{1,0:T(8,128)S(1)} %pad_add_fusion.pack.pack_ref.b_lists, s32[8,48]{1,0:T(8,128)S(1)} %collective-permute-done.2.c_lists, bf16[1024,128]{1,0:T(8,128)(2,1)S(1)} %collective-permute-done.4.a_ref, ...), custom_call_target="tpu_custom_call" | custom-call | flops 10000000000 | tf_op jit(solution)/shard_map/step1_part1/pallas_call | solution.py:157
  48.7 1.9 %collective-permute-start.5 = (s16[528,256]{1,0:T(8,128)(2,1)S(1)}, s16[528,256]{1,0:T(8,128)(2,1)S(1)}, u32[]{:S(2)}, u32[]{:S(2)}) collective-permute-start(s16[528,256]{1,0:T(8,128)(2,1)S(1)} %step1_part1.1), channel_id=1, source_target_pairs={{0,481},{1,480},{2,483},{3,482},{4,485},{5,484},{6,487},{7,486},{8... | collective-permute-start | bytes 811016 | tf_op jit(solution)/shard_map/send_c1/ppermute | solution.py:203
  50.6 7.9 %collective-permute-done.7.a_ref = bf16[1024,128]{1,0:T(8,128)(2,1)S(1)} collective-permute-done((bf16[1024,128]{1,0:T(8,128)(2,1)S(1)}, bf16[1024,128]{1,0:T(8,128)(2,1)S(1)}, u32[]{:S(2)}, u32[]{:S(2)}) %collective-permute-start.7) | collective-permute-done | bytes 262176 | tf_op jit(solution)/shard_map/send_a2/ppermute | solution.py:203
  58.5 1.2 %step1_part2.1 = s16[528,256]{1,0:T(8,128)(2,1)S(1)} custom-call(s32[1]{0:T(128)} %bitcast.14.first, s32[16,48]{1,0:T(8,128)S(1)} %slice_convert_fusion.a_lists, s32[8,48]{1,0:T(8,128)S(1)} %pad_add_fusion.pack.pack_ref.b_lists, s32[8,48]{1,0:T(8,128)S(1)} %collective-permute-done.2.c_lists, bf16[1024,128]{1,0:T(8,128)(2,1)S(1)} %collective-permute-done.7.a_ref, ...), custom_call_target="tpu_custom_call" | custom-call | flops 10000000000 | tf_op jit(solution)/shard_map/step1_part2/pallas_call | solution.py:157
  59.7 1.9 %collective-permute-start.9 = (s16[528,256]{1,0:T(8,128)(2,1)S(1)}, s16[528,256]{1,0:T(8,128)(2,1)S(1)}, u32[]{:S(2)}, u32[]{:S(2)}) collective-permute-start(s16[528,256]{1,0:T(8,128)(2,1)S(1)} %step1_part2.1), channel_id=1, source_target_pairs={{0,480},{1,481},{2,482},{3,483},{4,484},{5,485},{6,486},{7,487},{8... | collective-permute-start | bytes 811016 | tf_op jit(solution)/shard_map/send_c2/ppermute | solution.py:203
  61.6 3.5 %collective-permute-done.6.a_ref = bf16[1024,128]{1,0:T(8,128)(2,1)S(1)} collective-permute-done((bf16[1024,128]{1,0:T(8,128)(2,1)S(1)}, bf16[1024,128]{1,0:T(8,128)(2,1)S(1)}, u32[]{:S(2)}, u32[]{:S(2)}) %collective-permute-start.6) | collective-permute-done | bytes 262176 | tf_op jit(solution)/shard_map/send_a3/ppermute | solution.py:203
  65.1 1.2 %step1_part3.1 = s16[528,256]{1,0:T(8,128)(2,1)S(1)} custom-call(s32[1]{0:T(128)} %bitcast.13.first, s32[16,48]{1,0:T(8,128)S(1)} %slice_convert_fusion.a_lists, s32[8,48]{1,0:T(8,128)S(1)} %pad_add_fusion.pack.pack_ref.b_lists, s32[8,48]{1,0:T(8,128)S(1)} %collective-permute-done.2.c_lists, bf16[1024,128]{1,0:T(8,128)(2,1)S(1)} %collective-permute-done.6.a_ref, ...), custom_call_target="tpu_custom_call" | custom-call | flops 10000000000 | tf_op jit(solution)/shard_map/step1_part3/pallas_call | solution.py:157
  66.3 3.2 %collective-permute-start.10 = (s16[528,256]{1,0:T(8,128)(2,1)S(1)}, s16[528,256]{1,0:T(8,128)(2,1)S(1)}, u32[]{:S(2)}, u32[]{:S(2)}) collective-permute-start(s16[528,256]{1,0:T(8,128)(2,1)S(1)} %step1_part3.1), channel_id=1, source_target_pairs={{0,480},{1,481},{2,482},{3,483},{4,484},{5,485},{6,486},{7,487},{8... | collective-permute-start | bytes 811016 | tf_op jit(solution)/shard_map/send_c3/ppermute | solution.py:203
  69.5 1.3 %collective-permute-start.8 = (s16[1040,256]{1,0:T(8,128)(2,1)S(1)}, s16[1040,256]{1,0:T(8,128)(2,1)S(1)}, u32[]{:S(2)}, u32[]{:S(2)}) collective-permute-start(s16[1040,256]{1,0:T(8,128)(2,1)S(1)} %get-tuple-element.36), channel_id=1, source_target_pairs={{0,1},{2,3},{4,5},{6,7},{8,9},{10,11},{12,13},{14,15},{16,17},{18,... | collective-permute-start | bytes 1597448 | tf_op jit(solution)/shard_map/send_layer_up/ppermute | solution.py:203
  70.8 0.0 collective-permute-done.3.part_ref
  70.9 0.2 sum_part0.1.low_ref
  71.0 2.4 %collective-permute-done.5.part_ref = s16[528,256]{1,0:T(8,128)(2,1)S(1)} collective-permute-done((s16[528,256]{1,0:T(8,128)(2,1)S(1)}, s16[528,256]{1,0:T(8,128)(2,1)S(1)}, u32[]{:S(2)}, u32[]{:S(2)}) %collective-permute-start.5) | collective-permute-done | bytes 270368 | tf_op jit(solution)/shard_map/send_c1/ppermute | solution.py:203
  73.4 0.2 sum_part1.1.high_ref
  73.6 7.5 %collective-permute-done.9.part_ref = s16[528,256]{1,0:T(8,128)(2,1)S(1)} collective-permute-done((s16[528,256]{1,0:T(8,128)(2,1)S(1)}, s16[528,256]{1,0:T(8,128)(2,1)S(1)}, u32[]{:S(2)}, u32[]{:S(2)}) %collective-permute-start.9) | collective-permute-done | bytes 270368 | tf_op jit(solution)/shard_map/send_c2/ppermute | solution.py:203
  81.0 0.0 collective-permute-done.8.layer_ref
  81.0 1.0 %sum_part2.1 = (bf16[8,2,128,128]{3,2,1,0:T(8,128)(2,1)}, f32[512,256]{1,0:T(8,128)S(1)}) custom-call(s32[1]{0:T(128)} %bitcast.half, f32[512,256]{1,0:T(8,128)S(1)} %sum_part0.1.low_ref, f32[512,256]{1,0:T(8,128)S(1)} %sum_part1.1.high_ref, s16[1040,256]{1,0:T(8,128)(2,1)S(1)} %collective-permute-done.8.layer_ref, ...), custom_call_target="tpu_custom_call" | custom-call | flops 10000000000 | tf_op jit(solution)/shard_map/sum_part2/pallas_call | solution.py:157
  82.0 12.7 %collective-permute-done.10.part_ref = s16[528,256]{1,0:T(8,128)(2,1)S(1)} collective-permute-done((s16[528,256]{1,0:T(8,128)(2,1)S(1)}, s16[528,256]{1,0:T(8,128)(2,1)S(1)}, u32[]{:S(2)}, u32[]{:S(2)}) %collective-permute-start.10) | collective-permute-done | bytes 270368 | tf_op jit(solution)/shard_map/send_c3/ppermute | solution.py:203
  94.7 0.8 sum_part3.1
  (2 shorter events, 0.0 us)
Async XLA Ops:
  0.8 1.2 %copy-start = (bf16[1,1,1,16,2,128,128]{6,5,4,3,2,1,0:T(8,128)(2,1)S(1)}, bf16[1,1,1,16,2,128,128]{6,5,4,3,2,1,0:T(8,128)(2,1)}, u32[]{:S(2)}) copy-start(bf16[1,1,1,16,2,128,128]{6,5,4,3,2,1,0:T(8,128)(2,1)} %param.7) | copy-start | bytes 3145732
  2.0 32.1 %collective-permute-start.1 = (bf16[1040,128]{1,0:T(8,128)(2,1)S(1)}, bf16[1040,128]{1,0:T(8,128)(2,1)S(1)}, u32[]{:S(2)}, u32[]{:S(2)}) collective-permute-start(bf16[1040,128]{1,0:T(8,128)(2,1)S(1)} %head.1), channel_id=1, source_target_pairs={{0,62},{1,63},{2,32},{3,33},{4,34},{5,35},{6,36},{7,37},{8,38},{9,... | collective-permute-start | bytes 798728 | tf_op jit(solution)/shard_map/send_a0/ppermute | solution.py:203
  11.7 1.2 %copy-start.1 = (bf16[1,1,1,16,2,128,128]{6,5,4,3,2,1,0:T(8,128)(2,1)S(1)}, bf16[1,1,1,16,2,128,128]{6,5,4,3,2,1,0:T(8,128)(2,1)}, u32[]{:S(2)}) copy-start(bf16[1,1,1,16,2,128,128]{6,5,4,3,2,1,0:T(8,128)(2,1)} %param.7) | copy-start | bytes 3145732
  12.9 1.9 %copy-start.2 = (bf16[1,1,1,48,2,128,128]{6,5,4,3,2,1,0:T(8,128)(2,1)S(1)}, bf16[1,1,1,48,2,128,128]{6,5,4,3,2,1,0:T(8,128)(2,1)}, u32[]{:S(2)}) copy-start(bf16[1,1,1,48,2,128,128]{6,5,4,3,2,1,0:T(8,128)(2,1)} %param.10) | copy-start | bytes 9437188
  16.3 6.6 %collective-permute-start.2 = (s32[8,48]{1,0:T(8,128)S(1)}, s32[8,48]{1,0:T(8,128)S(1)}, u32[]{:S(2)}, u32[]{:S(2)}) collective-permute-start(s32[8,48]{1,0:T(8,128)S(1)} %pad_add_fusion.pack.pack_ref.b_lists), channel_id=1, source_target_pairs={{0,32},{1,33},{2,34},{3,35},{4,36},{5,37},{6,38},{7,39},{8,40},{9,... | collective-permute-start | bytes 4616 | tf_op jit(solution)/shard_map/send_c_cols/ppermute | solution.py:203
  20.8 26.7 %collective-permute-start = (s16[1040,256]{1,0:T(8,128)(2,1)S(1)}, s16[1040,256]{1,0:T(8,128)(2,1)S(1)}, u32[]{:S(2)}, u32[]{:S(2)}) collective-permute-start(s16[1040,256]{1,0:T(8,128)(2,1)S(1)} %get-tuple-element.36), channel_id=1, source_target_pairs={{1,0},{3,2},{5,4},{7,6},{9,8},{11,10},{13,12},{15,14},{17,16},{19,... | collective-permute-start | bytes 1597448 | tf_op jit(solution)/shard_map/send_layer_down/ppermute | solution.py:203
  22.9 24.6 %collective-permute-start.4 = (bf16[1024,128]{1,0:T(8,128)(2,1)S(1)}, bf16[1024,128]{1,0:T(8,128)(2,1)S(1)}, u32[]{:S(2)}, u32[]{:S(2)}) collective-permute-start(bf16[1024,128]{1,0:T(8,128)(2,1)S(1)} %get-tuple-element.28), channel_id=1, source_target_pairs={{0,62},{1,63},{2,32},{3,33},{4,34},{5,35},{6,36},{7,37},{8,38},{9,... | collective-permute-start | bytes 786440 | tf_op jit(solution)/shard_map/send_a1/ppermute | solution.py:203
  29.7 28.8 %collective-permute-start.7 = (bf16[1024,128]{1,0:T(8,128)(2,1)S(1)}, bf16[1024,128]{1,0:T(8,128)(2,1)S(1)}, u32[]{:S(2)}, u32[]{:S(2)}) collective-permute-start(bf16[1024,128]{1,0:T(8,128)(2,1)S(1)} %get-tuple-element.33), channel_id=1, source_target_pairs={{0,62},{1,63},{2,32},{3,33},{4,34},{5,35},{6,36},{7,37},{8,38},{9,... | collective-permute-start | bytes 786440 | tf_op jit(solution)/shard_map/send_a2/ppermute | solution.py:203
  34.2 1.9 %copy-start.3 = (bf16[1,1,1,48,2,128,128]{6,5,4,3,2,1,0:T(8,128)(2,1)S(1)}, bf16[1,1,1,48,2,128,128]{6,5,4,3,2,1,0:T(8,128)(2,1)}, u32[]{:S(2)}) copy-start(bf16[1,1,1,48,2,128,128]{6,5,4,3,2,1,0:T(8,128)(2,1)} %param.10) | copy-start | bytes 9437188
  37.3 33.6 %collective-permute-start.3 = (s16[528,256]{1,0:T(8,128)(2,1)S(1)}, s16[528,256]{1,0:T(8,128)(2,1)S(1)}, u32[]{:S(2)}, u32[]{:S(2)}) collective-permute-start(s16[528,256]{1,0:T(8,128)(2,1)S(1)} %step1_part0.1), channel_id=1, source_target_pairs={{0,481},{1,480},{2,483},{3,482},{4,485},{5,484},{6,487},{7,486},{8... | collective-permute-start | bytes 811016 | tf_op jit(solution)/shard_map/send_c0/ppermute | solution.py:203
  42.5 22.6 %collective-permute-start.6 = (bf16[1024,128]{1,0:T(8,128)(2,1)S(1)}, bf16[1024,128]{1,0:T(8,128)(2,1)S(1)}, u32[]{:S(2)}, u32[]{:S(2)}) collective-permute-start(bf16[1024,128]{1,0:T(8,128)(2,1)S(1)} %get-tuple-element.31), channel_id=1, source_target_pairs={{0,62},{1,63},{2,32},{3,33},{4,34},{5,35},{6,36},{7,37},{8,38},{9,... | collective-permute-start | bytes 786440 | tf_op jit(solution)/shard_map/send_a3/ppermute | solution.py:203
  48.7 24.7 %collective-permute-start.5 = (s16[528,256]{1,0:T(8,128)(2,1)S(1)}, s16[528,256]{1,0:T(8,128)(2,1)S(1)}, u32[]{:S(2)}, u32[]{:S(2)}) collective-permute-start(s16[528,256]{1,0:T(8,128)(2,1)S(1)} %step1_part1.1), channel_id=1, source_target_pairs={{0,481},{1,480},{2,483},{3,482},{4,485},{5,484},{6,487},{7,486},{8... | collective-permute-start | bytes 811016 | tf_op jit(solution)/shard_map/send_c1/ppermute | solution.py:203
  59.7 21.3 %collective-permute-start.9 = (s16[528,256]{1,0:T(8,128)(2,1)S(1)}, s16[528,256]{1,0:T(8,128)(2,1)S(1)}, u32[]{:S(2)}, u32[]{:S(2)}) collective-permute-start(s16[528,256]{1,0:T(8,128)(2,1)S(1)} %step1_part2.1), channel_id=1, source_target_pairs={{0,480},{1,481},{2,482},{3,483},{4,484},{5,485},{6,486},{7,487},{8... | collective-permute-start | bytes 811016 | tf_op jit(solution)/shard_map/send_c2/ppermute | solution.py:203
  66.3 28.4 %collective-permute-start.10 = (s16[528,256]{1,0:T(8,128)(2,1)S(1)}, s16[528,256]{1,0:T(8,128)(2,1)S(1)}, u32[]{:S(2)}, u32[]{:S(2)}) collective-permute-start(s16[528,256]{1,0:T(8,128)(2,1)S(1)} %step1_part3.1), channel_id=1, source_target_pairs={{0,480},{1,481},{2,482},{3,483},{4,484},{5,485},{6,486},{7,487},{8... | collective-permute-start | bytes 811016 | tf_op jit(solution)/shard_map/send_c3/ppermute | solution.py:203
  69.5 11.5 %collective-permute-start.8 = (s16[1040,256]{1,0:T(8,128)(2,1)S(1)}, s16[1040,256]{1,0:T(8,128)(2,1)S(1)}, u32[]{:S(2)}, u32[]{:S(2)}) collective-permute-start(s16[1040,256]{1,0:T(8,128)(2,1)S(1)} %get-tuple-element.36), channel_id=1, source_target_pairs={{0,1},{2,3},{4,5},{6,7},{8,9},{10,11},{12,13},{14,15},{16,17},{18,... | collective-permute-start | bytes 1597448 | tf_op jit(solution)/shard_map/send_layer_up/ppermute | solution.py:203

commit v3 on v2

--- a/solution.py
+++ b/solution.py
@@ -70,11 +70,12 @@
     numbers = []
     for k, value in enumerate(products):
         code, number = encode(value)
-        out_ref[pl.ds(k * BS, BS), :] = code
-        numbers.append(number)
+        for v in range(SLOTS_C):
+            out_ref[pl.ds((k * SLOTS_C + v) * BS, BS), :] = code[:, v * BS : (v + 1) * BS]
+            numbers.append(number[:, v * BS : (v + 1) * BS])
+    size = len(numbers) * BS
     numbers += [jnp.zeros_like(numbers[0])] * (TAIL - len(numbers))
-    tail = jnp.concatenate(numbers, axis=0)
-    out_ref[pl.ds(len(products) * BS, TAIL), :] = tail.astype(jnp.int16)
+    out_ref[pl.ds(size, TAIL), :] = jnp.concatenate(numbers, axis=0).astype(jnp.int16)
 
 
 def head_kernel(first, pack_ref, a_hbm, out_ref, tile, sem):
@@ -88,7 +89,7 @@
     copy.wait()
 
 
-def local_kernel(parts, half, pack, a_ref, b_ref, low_ref, high_ref, out_ref, *sent):
+def local_kernel(parts, half, pack, a_ref, b_ref, own_ref, out_ref, *sent):
     rows = a_ref.shape[0] // (2 * SLOTS_A * BS)
     other = (1 - half[0]) * rows
     own = half[0] * rows
@@ -99,8 +100,7 @@
         out_ref, [row_product(a_ref, other + k, b_ref, other + k, pack, pack, pack) for k in range(rows)]
     )
     for k in range(rows):
-        ref, at = (low_ref, k) if k < rows // 2 else (high_ref, k - rows // 2)
-        ref[pl.ds(at * BS, BS), :] = row_product(a_ref, own + k, b_ref, own + k, pack, pack, pack)
+        own_ref[pl.ds(k * BS, BS), :] = row_product(a_ref, own + k, b_ref, own + k, pack, pack, pack)
 
 
 def remote_kernel(first, a_lists, b_lists, c_lists, a_ref, b_ref, out_ref):
@@ -112,40 +112,47 @@
 
 
 def payload_row(ref, k):
-    rows = (ref.shape[0] - TAIL) // BS
-    tail = ref[pl.ds(rows * BS, TAIL), :].astype(jnp.int32)
-    return decode(ref[pl.ds(k * BS, BS), :], tail[k : k + 1, :])
-
-
-def add_kernel(start, wanted, half, total_ref, layer_ref, part_ref, out_ref):
-    rows = out_ref.shape[0] // BS
+    tail = ref[pl.ds(ref.shape[0] - TAIL, TAIL), :].astype(jnp.int32)
+    blocks = range(k * SLOTS_C, (k + 1) * SLOTS_C)
+    return jnp.concatenate([decode(ref[pl.ds(n * BS, BS), :], tail[n : n + 1, :]) for n in blocks], axis=1)
+
+
+def add_kernel(part, half, total_ref, part_ref, *refs):
+    *layer, out_ref = refs
+    _, start, count = part
+    for k in range(count):
+        at = pl.ds((start + k) * BS, BS)
+        out_ref[at, :] = total_ref[at, :] + payload_row(part_ref, k)
+    for layer_ref in layer:
+
+        @pl.when(half[0] == 0)
+        def _():
+            for k in range(out_ref.shape[0] // BS):
+                out_ref[pl.ds(k * BS, BS), :] += payload_row(layer_ref, k)
+
+
+def store_row(out_ref, k, total):
+    for v in range(SLOTS_C):
+        out_ref[k, v] = total[:, v * BS : (v + 1) * BS].astype(out_ref.dtype)
+
+
+def early_sum_kernel(part, kept, half, total_ref, layer_ref, part_ref, out_ref, rest_ref):
+    rows = out_ref.shape[0]
+    _, start, count = part
     for k in range(rows):
-        out_ref[pl.ds(k * BS, BS), :] = total_ref[pl.ds(k * BS, BS), :] + payload_row(part_ref, k)
-
-    @pl.when(half[0] == wanted)
-    def _():
-        for k in range(rows):
-            out_ref[pl.ds(k * BS, BS), :] += payload_row(layer_ref, start + k)
-
-
-def third_sum_kernel(half, low_ref, high_ref, layer_ref, part_ref, out_ref, rest_ref):
-    rows = low_ref.shape[0] // BS
-    slots = out_ref.shape[1]
-    scale = jnp.where(half[0] == 1, 1.0, 0.0)
-    for k in range(rows):
-        total = low_ref[pl.ds(k * BS, BS), :] + payload_row(part_ref, k)
+        total = total_ref[pl.ds(k * BS, BS), :]
+        if start <= k < start + count:
+            total = total + payload_row(part_ref, k - start)
         total = total + jnp.where(half[0] == 1, payload_row(layer_ref, k), 0.0)
-        for v in range(slots):
-            out_ref[k, v] = total[:, v * BS : (v + 1) * BS].astype(out_ref.dtype)
-        rest = jnp.where(half[0] == 1, payload_row(layer_ref, rows + k), 0.0)
-        rest_ref[pl.ds(k * BS, BS), :] = high_ref[pl.ds(k * BS, BS), :] + rest
+        if k < rows - kept:
+            store_row(out_ref, k, total)
+        else:
+            rest_ref[pl.ds((k - rows + kept) * BS, BS), :] = total
 
 
 def last_sum_kernel(rest_ref, part_ref, _, out_ref):
     for k in range(out_ref.shape[0]):
-        total = rest_ref[pl.ds(k * BS, BS), :] + payload_row(part_ref, k)
-        for v in range(out_ref.shape[1]):
-            out_ref[k, v] = total[:, v * BS : (v + 1) * BS].astype(out_ref.dtype)
+        store_row(out_ref, k, rest_ref[pl.ds(k * BS, BS), :] + payload_row(part_ref, k))
 
 
 SMEM = pl.BlockSpec(memory_space=pltpu.SMEM)
@@ -169,8 +176,9 @@
 PARTS = ((False, 0, 4), (False, 4, 4), (True, 0, 4), (True, 4, 4))
 US = 1e9
 COST_STEP0 = 2
-COST_STEP1 = 10
-COST_SUM = 10
+COST_STEP1 = 25
+COST_FIRST = 6
+COST_SUM = 1
 
 
 def after(value, *others):
@@ -186,11 +194,11 @@
     layer = lax.axis_index("layer").astype(jnp.int32)
     rows = a_panel.shape[0] // 2
     wide = out_cols.shape[1] * BS
-    summed = jax.ShapeDtypeStruct((rows // 2 * BS, wide), jnp.float32)
+    summed = jax.ShapeDtypeStruct((rows * BS, wide), jnp.float32)
     result = jax.ShapeDtypeStruct((rows, out_cols.shape[1], BS, BS), jnp.bfloat16)
 
     def coded(count):
-        return jax.ShapeDtypeStruct((count * BS + TAIL, wide), jnp.int16)
+        return jax.ShapeDtypeStruct((count * SLOTS_C * BS + TAIL, BS), jnp.int16)
 
     def place(i, j, l):
         return ((i % n_row) * n_col + j % n_col) * 2 + l
@@ -223,12 +231,11 @@
     far_a = [send("send_a0", head, to_user)]
 
     parts = PARTS[1:]
-    low, high, other, *a_parts = call(
+    own, other, *a_parts = call(
         functools.partial(local_kernel, parts),
         (half, pack),
         (a_panel, b_panel),
         (
-            summed,
             summed,
             coded(rows),
             *(jax.ShapeDtypeStruct((count * row_size, BS), a_panel.dtype) for _, _, count in parts),
@@ -238,7 +245,7 @@
     )
     down = send("send_layer_down", other, lambda i, j, l: (i, j, 0), who=(1,))
     far_cols = send("send_c_cols", after(pack, other), lambda i, j, l: (i + 1, j, l))
-    far_a += [send(f"send_a{k + 1}", after(part, far_cols), to_user) for k, part in enumerate(a_parts[:-1])]
+    far_a.append(send("send_a1", a_parts[0], to_user))
 
     far_lists = far_a[0][-TAIL:, : pack.shape[1]].astype(jnp.int32)
     back, before = [], []
@@ -248,30 +255,48 @@
             (first[None], far_lists, pack, far_cols),
             (after(far_a[k], *before), b_panel),
             coded(count),
-            COST_STEP1,
+            COST_FIRST if k == 0 else COST_STEP1,
             f"step1_part{k}",
         )
         before = [product]
         if k == 0:
             before.append(down)
-            far_a.append(send(f"send_a{len(far_a)}", after(a_parts[-1], product), to_user))
+        if k + 1 < len(a_parts):
+            far_a.append(send(f"send_a{k + 2}", after(a_parts[k + 1], product), to_user))
+        if k == len(PARTS) - 3:
+            up = send("send_layer_up", after(other, product), lambda i, j, l: (i, j, 1), who=(0,))
         back.append(send(f"send_c{k}", product, lambda i, j, l, same=same: (i - 1, j, l if same else 1 - l)))
-    up = send("send_layer_up", after(other, product), lambda i, j, l: (i, j, 1), who=(0,))
-
-    add = functools.partial(call, outs=summed, cost=COST_SUM)
-    low = add(functools.partial(add_kernel, 0, 0), (half,), (low, down, back[0]), name="sum_part0")
-    high = add(functools.partial(add_kernel, rows // 2, 0), (half,), (after(high, low), down, back[1]), name="sum_part1")
-    c, rest = call(third_sum_kernel, (half,), (low, high, up, back[2]), (result, summed), COST_SUM, "sum_part2")
+    total, more = own, (down,)
+    for k, part in enumerate(PARTS[:-2]):
+        total = call(
+            functools.partial(add_kernel, part),
+            (half,),
+            (total, back[k], *more),
+            summed,
+            COST_SUM,
+            f"sum_part{k}",
+            input_output_aliases={1: 0},
+        )
+        more = ()
+    kept = PARTS[-1][2]
+    rest = jax.ShapeDtypeStruct((kept * BS, wide), jnp.float32)
+    c, rest = call(
+        functools.partial(early_sum_kernel, PARTS[-2], kept), (half,), (total, up, back[-2]), (result, rest), COST_SUM, "sum_early"
+    )
     c = pl.pallas_call(
         last_sum_kernel,
         grid=(1,),
-        in_specs=[pl.BlockSpec(summed.shape, lambda _: (0, 0)), pl.BlockSpec(coded(rows // 2).shape, lambda _: (0, 0)), pl.BlockSpec(memory_space=pl.ANY)],
-        out_specs=pl.BlockSpec((rows // 2, *result.shape[1:]), lambda _: (1, 0, 0, 0)),
+        in_specs=[
+            pl.BlockSpec(rest.shape, lambda _: (0, 0)),
+            pl.BlockSpec(back[-1].shape, lambda _: (0, 0)),
+            pl.BlockSpec(memory_space=pl.ANY),
+        ],
+        out_specs=pl.BlockSpec((kept, *result.shape[1:]), lambda _: (rows // kept - 1, 0, 0, 0)),
         out_shape=result,
         input_output_aliases={2: 0},
         compiler_params=pltpu.CompilerParams(vmem_limit_bytes=VMEM_LIMIT),
-        name="sum_part3",
-    )(rest, back[3], c)
+        name="sum_last",
+    )(rest, back[-1], c)
     return c[None, None]
 
 

time: 96 us -> 90 us (0.938)
  the two profiles are of different devices: /device:TPU:54 before, /device:TPU:9 now
where the time goes in v3:
time: 90 us; the launch traced here: 89.5 us
  starting transfers between devices  52.7 us (59%)
  waiting for transfers between devices  20.3 us (23%)
  Pallas kernels  8.3 us (9%)
  local copies, waits for them, and re-layouts  7.19 us (8%)
    ppermute x11, starting transfers between devices, send(): return lax.ppermute(value, ('row', 'col', 'layer'), pairs)  52.7 us
    ppermute x11, waiting for transfers between devices, send(): return lax.ppermute(value, ('row', 'col', 'layer'), pairs)  20.3 us
    pallas_call x8, Pallas kernels, call(): pl.pallas_call(kernel, in_specs=[SMEM] * len(scalars) + [VMEM] * len(arra...  7.48 us
    unnamed x12, local copies, waits for them, and re-layouts  7.19 us
  transfers between devices with their start and end apart: 11, of which 4 were waited for; matrix products, arithmetic and copies ran while one was open for 0% of the time, Pallas kernels for 8%

profile of v3, /device:TPU:9, one launch (start us, length us, event | category | flops | bytes accessed | tf_op | source)
XLA Modules:
  0.0 89.5 jit_solution(1187506468760851109)
XLA Ops:
  0.0 0.8 pad_add_fusion.pack.pack_ref.b_lists
  0.8 0.0 copy-start
  0.8 1.2 %copy-done = bf16[1,1,1,16,2,128,128]{6,5,4,3,2,1,0:T(8,128)(2,1)S(1)} copy-done((bf16[1,1,1,16,2,128,128]{6,5,4,3,2,1,0:T(8,128)(2,1)S(1)}, bf16[1,1,1,16,2,128,128]{6,5,4,3,2,1,0:T(8,128)(2,1)}, u32[]{:S(2)}) %copy-start) | copy-done | bytes 1048600
  2.0 4.8 %collective-permute-start = (bf16[1040,128]{1,0:T(8,128)(2,1)S(1)}, bf16[1040,128]{1,0:T(8,128)(2,1)S(1)}, u32[]{:S(2)}, u32[]{:S(2)}) collective-permute-start(bf16[1040,128]{1,0:T(8,128)(2,1)S(1)} %head.1), channel_id=1, source_target_pairs={{0,62},{1,63},{2,32},{3,33},{4,34},{5,35},{6,36},{7,37},{8,38},{9,... | collective-permute-start | bytes 798728 | tf_op jit(solution)/shard_map/send_a0/ppermute | solution.py:211
  6.8 0.0 copy-start.1
  6.8 1.2 %copy-done.1 = bf16[1,1,1,16,2,128,128]{6,5,4,3,2,1,0:T(8,128)(2,1)S(1)} copy-done((bf16[1,1,1,16,2,128,128]{6,5,4,3,2,1,0:T(8,128)(2,1)S(1)}, bf16[1,1,1,16,2,128,128]{6,5,4,3,2,1,0:T(8,128)(2,1)}, u32[]{:S(2)}) %copy-start.1) | copy-done | bytes 1048600
  8.0 0.0 copy-start.2
  8.0 1.9 %copy-done.2 = bf16[1,1,1,48,2,128,128]{6,5,4,3,2,1,0:T(8,128)(2,1)S(1)} copy-done((bf16[1,1,1,48,2,128,128]{6,5,4,3,2,1,0:T(8,128)(2,1)S(1)}, bf16[1,1,1,48,2,128,128]{6,5,4,3,2,1,0:T(8,128)(2,1)}, u32[]{:S(2)}) %copy-start.2) | copy-done | bytes 3145752
  9.9 1.6 %step0.1 = (f32[1024,256]{1,0:T(8,128)S(1)}, s16[2064,128]{1,0:T(8,128)(2,1)S(1)}, bf16[1024,128]{1,0:T(8,128)(2,1)S(1)}, bf16[1024,128]{1,0:T(8,128)(2,1)S(1)}, bf16[1024,128]{1,0:T(8,128)(2,1)S(1)}) custom-call(s32[1]{0:T(128)} %bitcast.half, s32[8,48]{1,0:T(8,128)S(1)} %pad_add_fusion.pack.pack_ref.b_lists, bf16[4096,128]{1,0:T(8,128)(2,1)S(1)} %bitcast.20, ...), custom_call_target="tpu_custom_call" | custom-call | flops 2000000000 | tf_op jit(solution)/shard_map/step0/pallas_call | solution.py:164
  11.5 0.0 copy-start.4
  11.5 1.0 %copy-done.4 = f32[1024,256]{1,0:T(8,128)} copy-done((f32[1024,256]{1,0:T(8,128)}, f32[1024,256]{1,0:T(8,128)S(1)}, u32[]{:S(2)}) %copy-start.4) | copy-done | bytes 1048600
  12.5 2.1 %collective-permute-start.3 = (s16[2064,128]{1,0:T(8,128)(2,1)S(1)}, s16[2064,128]{1,0:T(8,128)(2,1)S(1)}, u32[]{:S(2)}, u32[]{:S(2)}) collective-permute-start(s16[2064,128]{1,0:T(8,128)(2,1)S(1)} %get-tuple-element.24), channel_id=1, source_target_pairs={{1,0},{3,2},{5,4},{7,6},{9,8},{11,10},{13,12},{15,14},{17,16},{19,... | collective-permute-start | bytes 1585160 | tf_op jit(solution)/shard_map/send_layer_down/ppermute | solution.py:211
  14.6 5.4 %collective-permute-start.1 = (s32[8,48]{1,0:T(8,128)S(1)}, s32[8,48]{1,0:T(8,128)S(1)}, u32[]{:S(2)}, u32[]{:S(2)}) collective-permute-start(s32[8,48]{1,0:T(8,128)S(1)} %pad_add_fusion.pack.pack_ref.b_lists), channel_id=1, source_target_pairs={{0,32},{1,33},{2,34},{3,35},{4,36},{5,37},{6,38},{7,39},{8,40},{9,... | collective-permute-start | bytes 4616 | tf_op jit(solution)/shard_map/send_c_cols/ppermute | solution.py:211
  20.0 11.2 %collective-permute-start.4 = (bf16[1024,128]{1,0:T(8,128)(2,1)S(1)}, bf16[1024,128]{1,0:T(8,128)(2,1)S(1)}, u32[]{:S(2)}, u32[]{:S(2)}) collective-permute-start(bf16[1024,128]{1,0:T(8,128)(2,1)S(1)} %get-tuple-element.22), channel_id=1, source_target_pairs={{0,62},{1,63},{2,32},{3,33},{4,34},{5,35},{6,36},{7,37},{8,38},{9,... | collective-permute-start | bytes 786440 | tf_op jit(solution)/shard_map/send_a1/ppermute | solution.py:211
  31.2 0.0 collective-permute-done.a_ref
  31.2 0.0 collective-permute-done.1.c_lists
  31.2 0.0 copy-start.3
  31.3 1.9 %copy-done.3 = bf16[1,1,1,48,2,128,128]{6,5,4,3,2,1,0:T(8,128)(2,1)S(1)} copy-done((bf16[1,1,1,48,2,128,128]{6,5,4,3,2,1,0:T(8,128)(2,1)S(1)}, bf16[1,1,1,48,2,128,128]{6,5,4,3,2,1,0:T(8,128)(2,1)}, u32[]{:S(2)}) %copy-start.3) | copy-done | bytes 3145752
  33.1 1.2 %step1_part0.1 = s16[1040,128]{1,0:T(8,128)(2,1)S(1)} custom-call(s32[1]{0:T(128)} %bitcast.11.first, s32[16,48]{1,0:T(8,128)S(1)} %slice_convert_fusion.a_lists, s32[8,48]{1,0:T(8,128)S(1)} %pad_add_fusion.pack.pack_ref.b_lists, s32[8,48]{1,0:T(8,128)S(1)} %collective-permute-done.1.c_lists, bf16[1040,128]{1,0:T(8,128)(2,1)S(1)} %collective-permute-done.a_ref, ...), custom_call_target="tpu_custom_call" | custom-call | flops 6000000000 | tf_op jit(solution)/shard_map/step1_part0/pallas_call | solution.py:164
  34.3 5.9 %collective-permute-start.2 = (s16[1040,128]{1,0:T(8,128)(2,1)S(1)}, s16[1040,128]{1,0:T(8,128)(2,1)S(1)}, u32[]{:S(2)}, u32[]{:S(2)}) collective-permute-start(s16[1040,128]{1,0:T(8,128)(2,1)S(1)} %step1_part0.1), channel_id=1, source_target_pairs={{0,481},{1,480},{2,483},{3,482},{4,485},{5,484},{6,487},{7,486},{8... | collective-permute-start | bytes 798728 | tf_op jit(solution)/shard_map/send_c0/ppermute | solution.py:211
  40.2 1.9 %collective-permute-start.7 = (bf16[1024,128]{1,0:T(8,128)(2,1)S(1)}, bf16[1024,128]{1,0:T(8,128)(2,1)S(1)}, u32[]{:S(2)}, u32[]{:S(2)}) collective-permute-start(bf16[1024,128]{1,0:T(8,128)(2,1)S(1)} %get-tuple-element.26), channel_id=1, source_target_pairs={{0,62},{1,63},{2,32},{3,33},{4,34},{5,35},{6,36},{7,37},{8,38},{9,... | collective-permute-start | bytes 786440 | tf_op jit(solution)/shard_map/send_a2/ppermute | solution.py:211
  42.1 0.0 collective-permute-done.4.a_ref
  42.2 0.0 collective-permute-done.3.refs_0_
  42.2 1.2 %step1_part1.1 = s16[1040,128]{1,0:T(8,128)(2,1)S(1)} custom-call(s32[1]{0:T(128)} %bitcast.12.first, s32[16,48]{1,0:T(8,128)S(1)} %slice_convert_fusion.a_lists, s32[8,48]{1,0:T(8,128)S(1)} %pad_add_fusion.pack.pack_ref.b_lists, s32[8,48]{1,0:T(8,128)S(1)} %collective-permute-done.1.c_lists, bf16[1024,128]{1,0:T(8,128)(2,1)S(1)} %collective-permute-done.4.a_ref, ...), custom_call_target="tpu_custom_call" | custom-call | flops 24999999488 | tf_op jit(solution)/shard_map/step1_part1/pallas_call | solution.py:164
  43.4 9.1 %collective-permute-start.5 = (s16[1040,128]{1,0:T(8,128)(2,1)S(1)}, s16[1040,128]{1,0:T(8,128)(2,1)S(1)}, u32[]{:S(2)}, u32[]{:S(2)}) collective-permute-start(s16[1040,128]{1,0:T(8,128)(2,1)S(1)} %step1_part1.1), channel_id=1, source_target_pairs={{0,481},{1,480},{2,483},{3,482},{4,485},{5,484},{6,487},{7,486},{8... | collective-permute-start | bytes 798728 | tf_op jit(solution)/shard_map/send_c1/ppermute | solution.py:211
  52.5 3.5 %collective-permute-start.9 = (bf16[1024,128]{1,0:T(8,128)(2,1)S(1)}, bf16[1024,128]{1,0:T(8,128)(2,1)S(1)}, u32[]{:S(2)}, u32[]{:S(2)}) collective-permute-start(bf16[1024,128]{1,0:T(8,128)(2,1)S(1)} %get-tuple-element.30), channel_id=1, source_target_pairs={{0,62},{1,63},{2,32},{3,33},{4,34},{5,35},{6,36},{7,37},{8,38},{9,... | collective-permute-start | bytes 786440 | tf_op jit(solution)/shard_map/send_a3/ppermute | solution.py:211
  56.0 0.6 collective-permute-done.7.a_ref
  56.6 1.2 %step1_part2.1 = s16[1040,128]{1,0:T(8,128)(2,1)S(1)} custom-call(s32[1]{0:T(128)} %bitcast.13.first, s32[16,48]{1,0:T(8,128)S(1)} %slice_convert_fusion.a_lists, s32[8,48]{1,0:T(8,128)S(1)} %pad_add_fusion.pack.pack_ref.b_lists, s32[8,48]{1,0:T(8,128)S(1)} %collective-permute-done.1.c_lists, bf16[1024,128]{1,0:T(8,128)(2,1)S(1)} %collective-permute-done.7.a_ref, ...), custom_call_target="tpu_custom_call" | custom-call | flops 24999999488 | tf_op jit(solution)/shard_map/step1_part2/pallas_call | solution.py:164
  57.8 5.6 %collective-permute-start.8 = (s16[1040,128]{1,0:T(8,128)(2,1)S(1)}, s16[1040,128]{1,0:T(8,128)(2,1)S(1)}, u32[]{:S(2)}, u32[]{:S(2)}) collective-permute-start(s16[1040,128]{1,0:T(8,128)(2,1)S(1)} %step1_part2.1), channel_id=1, source_target_pairs={{0,480},{1,481},{2,482},{3,483},{4,484},{5,485},{6,486},{7,487},{8... | collective-permute-start | bytes 798728 | tf_op jit(solution)/shard_map/send_c2/ppermute | solution.py:211
  63.4 1.3 %collective-permute-start.6 = (s16[2064,128]{1,0:T(8,128)(2,1)S(1)}, s16[2064,128]{1,0:T(8,128)(2,1)S(1)}, u32[]{:S(2)}, u32[]{:S(2)}) collective-permute-start(s16[2064,128]{1,0:T(8,128)(2,1)S(1)} %get-tuple-element.24), channel_id=1, source_target_pairs={{0,1},{2,3},{4,5},{6,7},{8,9},{10,11},{12,13},{14,15},{16,17},{18,... | collective-permute-start | bytes 1585160 | tf_op jit(solution)/shard_map/send_layer_up/ppermute | solution.py:211
  64.7 7.8 %collective-permute-done.9.a_ref = bf16[1024,128]{1,0:T(8,128)(2,1)S(1)} collective-permute-done((bf16[1024,128]{1,0:T(8,128)(2,1)S(1)}, bf16[1024,128]{1,0:T(8,128)(2,1)S(1)}, u32[]{:S(2)}, u32[]{:S(2)}) %collective-permute-start.9) | collective-permute-done | bytes 262176 | tf_op jit(solution)/shard_map/send_a3/ppermute | solution.py:211
  72.5 0.0 copy-start.5
  72.5 1.2 %step1_part3.1 = s16[1040,128]{1,0:T(8,128)(2,1)S(1)} custom-call(s32[1]{0:T(128)} %bitcast.14.first, s32[16,48]{1,0:T(8,128)S(1)} %slice_convert_fusion.a_lists, s32[8,48]{1,0:T(8,128)S(1)} %pad_add_fusion.pack.pack_ref.b_lists, s32[8,48]{1,0:T(8,128)S(1)} %collective-permute-done.1.c_lists, bf16[1024,128]{1,0:T(8,128)(2,1)S(1)} %collective-permute-done.9.a_ref, ...), custom_call_target="tpu_custom_call" | custom-call | flops 24999999488 | tf_op jit(solution)/shard_map/step1_part3/pallas_call | solution.py:164
  73.7 1.9 %collective-permute-start.10 = (s16[1040,128]{1,0:T(8,128)(2,1)S(1)}, s16[1040,128]{1,0:T(8,128)(2,1)S(1)}, u32[]{:S(2)}, u32[]{:S(2)}) collective-permute-start(s16[1040,128]{1,0:T(8,128)(2,1)S(1)} %step1_part3.1), channel_id=1, source_target_pairs={{0,480},{1,481},{2,482},{3,483},{4,484},{5,485},{6,486},{7,487},{8... | collective-permute-start | bytes 798728 | tf_op jit(solution)/shard_map/send_c3/ppermute | solution.py:211
  75.7 0.0 collective-permute-done.2.part_ref
  75.7 0.0 copy-done.5
  75.7 0.1 sum_part0.1.total_ref
  75.8 0.0 collective-permute-done.5.part_ref
  75.8 0.1 sum_part1.1.total_ref
  75.9 0.0 collective-permute-done.8.part_ref
  75.9 2.7 %collective-permute-done.6.layer_ref = s16[2064,128]{1,0:T(8,128)(2,1)S(1)} collective-permute-done((s16[2064,128]{1,0:T(8,128)(2,1)S(1)}, s16[2064,128]{1,0:T(8,128)(2,1)S(1)}, u32[]{:S(2)}, u32[]{:S(2)}) %collective-permute-start.6) | collective-permute-done | bytes 528416 | tf_op jit(solution)/shard_map/send_layer_up/ppermute | solution.py:211
  78.6 1.0 %sum_early.1 = (bf16[8,2,128,128]{3,2,1,0:T(8,128)(2,1)}, f32[512,256]{1,0:T(8,128)S(1)}) custom-call(s32[1]{0:T(128)} %bitcast.half, f32[1024,256]{1,0:T(8,128)S(1)} %sum_part1.1.total_ref, s16[2064,128]{1,0:T(8,128)(2,1)S(1)} %collective-permute-done.6.layer_ref, s16[1040,128]{1,0:T(8,128)(2,1)S(1)} %collective-permute-done.8.part_ref), custom_call_target="tpu_custom_call" | custom-call | flops 1000000000 | tf_op jit(solution)/shard_map/sum_early/pallas_call | solution.py:164
  79.6 9.1 %collective-permute-done.10.part_ref = s16[1040,128]{1,0:T(8,128)(2,1)S(1)} collective-permute-done((s16[1040,128]{1,0:T(8,128)(2,1)S(1)}, s16[1040,128]{1,0:T(8,128)(2,1)S(1)}, u32[]{:S(2)}, u32[]{:S(2)}) %collective-permute-start.10) | collective-permute-done | bytes 266272 | tf_op jit(solution)/shard_map/send_c3/ppermute | solution.py:211
  88.7 0.8 sum_last.1
  (2 shorter events, 0.0 us)
Async XLA Ops:
  0.8 1.2 %copy-start = (bf16[1,1,1,16,2,128,128]{6,5,4,3,2,1,0:T(8,128)(2,1)S(1)}, bf16[1,1,1,16,2,128,128]{6,5,4,3,2,1,0:T(8,128)(2,1)}, u32[]{:S(2)}) copy-start(bf16[1,1,1,16,2,128,128]{6,5,4,3,2,1,0:T(8,128)(2,1)} %param.7) | copy-start | bytes 3145732
  2.0 29.2 %collective-permute-start = (bf16[1040,128]{1,0:T(8,128)(2,1)S(1)}, bf16[1040,128]{1,0:T(8,128)(2,1)S(1)}, u32[]{:S(2)}, u32[]{:S(2)}) collective-permute-start(bf16[1040,128]{1,0:T(8,128)(2,1)S(1)} %head.1), channel_id=1, source_target_pairs={{0,62},{1,63},{2,32},{3,33},{4,34},{5,35},{6,36},{7,37},{8,38},{9,... | collective-permute-start | bytes 798728 | tf_op jit(solution)/shard_map/send_a0/ppermute | solution.py:211
  6.8 1.2 %copy-start.1 = (bf16[1,1,1,16,2,128,128]{6,5,4,3,2,1,0:T(8,128)(2,1)S(1)}, bf16[1,1,1,16,2,128,128]{6,5,4,3,2,1,0:T(8,128)(2,1)}, u32[]{:S(2)}) copy-start(bf16[1,1,1,16,2,128,128]{6,5,4,3,2,1,0:T(8,128)(2,1)} %param.7) | copy-start | bytes 3145732
  8.0 1.9 %copy-start.2 = (bf16[1,1,1,48,2,128,128]{6,5,4,3,2,1,0:T(8,128)(2,1)S(1)}, bf16[1,1,1,48,2,128,128]{6,5,4,3,2,1,0:T(8,128)(2,1)}, u32[]{:S(2)}) copy-start(bf16[1,1,1,48,2,128,128]{6,5,4,3,2,1,0:T(8,128)(2,1)} %param.10) | copy-start | bytes 9437188
  11.5 1.0 %copy-start.4 = (f32[1024,256]{1,0:T(8,128)}, f32[1024,256]{1,0:T(8,128)S(1)}, u32[]{:S(2)}) copy-start(f32[1024,256]{1,0:T(8,128)S(1)} %get-tuple-element.19.total_ref) | copy-start | bytes 3145732
  12.5 29.7 %collective-permute-start.3 = (s16[2064,128]{1,0:T(8,128)(2,1)S(1)}, s16[2064,128]{1,0:T(8,128)(2,1)S(1)}, u32[]{:S(2)}, u32[]{:S(2)}) collective-permute-start(s16[2064,128]{1,0:T(8,128)(2,1)S(1)} %get-tuple-element.24), channel_id=1, source_target_pairs={{1,0},{3,2},{5,4},{7,6},{9,8},{11,10},{13,12},{15,14},{17,16},{19,... | collective-permute-start | bytes 1585160 | tf_op jit(solution)/shard_map/send_layer_down/ppermute | solution.py:211
  14.6 16.7 %collective-permute-start.1 = (s32[8,48]{1,0:T(8,128)S(1)}, s32[8,48]{1,0:T(8,128)S(1)}, u32[]{:S(2)}, u32[]{:S(2)}) collective-permute-start(s32[8,48]{1,0:T(8,128)S(1)} %pad_add_fusion.pack.pack_ref.b_lists), channel_id=1, source_target_pairs={{0,32},{1,33},{2,34},{3,35},{4,36},{5,37},{6,38},{7,39},{8,40},{9,... | collective-permute-start | bytes 4616 | tf_op jit(solution)/shard_map/send_c_cols/ppermute | solution.py:211
  20.0 22.1 %collective-permute-start.4 = (bf16[1024,128]{1,0:T(8,128)(2,1)S(1)}, bf16[1024,128]{1,0:T(8,128)(2,1)S(1)}, u32[]{:S(2)}, u32[]{:S(2)}) collective-permute-start(bf16[1024,128]{1,0:T(8,128)(2,1)S(1)} %get-tuple-element.22), channel_id=1, source_target_pairs={{0,62},{1,63},{2,32},{3,33},{4,34},{5,35},{6,36},{7,37},{8,38},{9,... | collective-permute-start | bytes 786440 | tf_op jit(solution)/shard_map/send_a1/ppermute | solution.py:211
  31.2 1.9 %copy-start.3 = (bf16[1,1,1,48,2,128,128]{6,5,4,3,2,1,0:T(8,128)(2,1)S(1)}, bf16[1,1,1,48,2,128,128]{6,5,4,3,2,1,0:T(8,128)(2,1)}, u32[]{:S(2)}) copy-start(bf16[1,1,1,48,2,128,128]{6,5,4,3,2,1,0:T(8,128)(2,1)} %param.10) | copy-start | bytes 9437188
  34.3 41.3 %collective-permute-start.2 = (s16[1040,128]{1,0:T(8,128)(2,1)S(1)}, s16[1040,128]{1,0:T(8,128)(2,1)S(1)}, u32[]{:S(2)}, u32[]{:S(2)}) collective-permute-start(s16[1040,128]{1,0:T(8,128)(2,1)S(1)} %step1_part0.1), channel_id=1, source_target_pairs={{0,481},{1,480},{2,483},{3,482},{4,485},{5,484},{6,487},{7,486},{8... | collective-permute-start | bytes 798728 | tf_op jit(solution)/shard_map/send_c0/ppermute | solution.py:211
  40.2 16.4 %collective-permute-start.7 = (bf16[1024,128]{1,0:T(8,128)(2,1)S(1)}, bf16[1024,128]{1,0:T(8,128)(2,1)S(1)}, u32[]{:S(2)}, u32[]{:S(2)}) collective-permute-start(bf16[1024,128]{1,0:T(8,128)(2,1)S(1)} %get-tuple-element.26), channel_id=1, source_target_pairs={{0,62},{1,63},{2,32},{3,33},{4,34},{5,35},{6,36},{7,37},{8,38},{9,... | collective-permute-start | bytes 786440 | tf_op jit(solution)/shard_map/send_a2/ppermute | solution.py:211
  43.4 32.4 %collective-permute-start.5 = (s16[1040,128]{1,0:T(8,128)(2,1)S(1)}, s16[1040,128]{1,0:T(8,128)(2,1)S(1)}, u32[]{:S(2)}, u32[]{:S(2)}) collective-permute-start(s16[1040,128]{1,0:T(8,128)(2,1)S(1)} %step1_part1.1), channel_id=1, source_target_pairs={{0,481},{1,480},{2,483},{3,482},{4,485},{5,484},{6,487},{7,486},{8... | collective-permute-start | bytes 798728 | tf_op jit(solution)/shard_map/send_c1/ppermute | solution.py:211
  52.5 20.1 %collective-permute-start.9 = (bf16[1024,128]{1,0:T(8,128)(2,1)S(1)}, bf16[1024,128]{1,0:T(8,128)(2,1)S(1)}, u32[]{:S(2)}, u32[]{:S(2)}) collective-permute-start(bf16[1024,128]{1,0:T(8,128)(2,1)S(1)} %get-tuple-element.30), channel_id=1, source_target_pairs={{0,62},{1,63},{2,32},{3,33},{4,34},{5,35},{6,36},{7,37},{8,38},{9,... | collective-permute-start | bytes 786440 | tf_op jit(solution)/shard_map/send_a3/ppermute | solution.py:211
  57.8 18.1 %collective-permute-start.8 = (s16[1040,128]{1,0:T(8,128)(2,1)S(1)}, s16[1040,128]{1,0:T(8,128)(2,1)S(1)}, u32[]{:S(2)}, u32[]{:S(2)}) collective-permute-start(s16[1040,128]{1,0:T(8,128)(2,1)S(1)} %step1_part2.1), channel_id=1, source_target_pairs={{0,480},{1,481},{2,482},{3,483},{4,484},{5,485},{6,486},{7,487},{8... | collective-permute-start | bytes 798728 | tf_op jit(solution)/shard_map/send_c2/ppermute | solution.py:211
  63.4 15.2 %collective-permute-start.6 = (s16[2064,128]{1,0:T(8,128)(2,1)S(1)}, s16[2064,128]{1,0:T(8,128)(2,1)S(1)}, u32[]{:S(2)}, u32[]{:S(2)}) collective-permute-start(s16[2064,128]{1,0:T(8,128)(2,1)S(1)} %get-tuple-element.24), channel_id=1, source_target_pairs={{0,1},{2,3},{4,5},{6,7},{8,9},{10,11},{12,13},{14,15},{16,17},{18,... | collective-permute-start | bytes 1585160 | tf_op jit(solution)/shard_map/send_layer_up/ppermute | solution.py:211
  72.5 3.1 %copy-start.5 = (f32[1024,256]{1,0:T(8,128)S(1)}, f32[1024,256]{1,0:T(8,128)}, u32[]{:S(2)}) copy-start(f32[1024,256]{1,0:T(8,128)} %copy-done.4) | copy-start | bytes 3145732
  73.7 15.0 %collective-permute-start.10 = (s16[1040,128]{1,0:T(8,128)(2,1)S(1)}, s16[1040,128]{1,0:T(8,128)(2,1)S(1)}, u32[]{:S(2)}, u32[]{:S(2)}) collective-permute-start(s16[1040,128]{1,0:T(8,128)(2,1)S(1)} %step1_part3.1), channel_id=1, source_target_pairs={{0,480},{1,481},{2,482},{3,483},{4,484},{5,485},{6,486},{7,487},{8... | collective-permute-start | bytes 798728 | tf_op jit(solution)/shard_map/send_c3/ppermute | solution.py:211

commit v4 on v3

--- a/solution.py
+++ b/solution.py
@@ -14,7 +14,7 @@
 TAIL = 16
 SLOTS_A, SLOTS_C = 2, 2
 B_COLS, B_COUNT, A_COLS, A_COUNT, C_COLS = 0, 2, 3, 5, 6
-VMEM_LIMIT = 16 * 1024 * 1024
+VMEM_LIMIT = 48 * 1024 * 1024
 
 
 def row_product(a_ref, a_row, b_ref, r, a_lists, b_lists, c_lists):

time: 90 us -> 89.2 us (level)
  local copies, waits for them, and re-layouts: 7.19 us -> 5.31 us
  Pallas kernels: 8.3 us -> 9.6 us
    unnamed x12 -> x10, local copies, waits for them, and re-layouts: 7.19 us -> 5.31 us
    pallas_call x8, Pallas kernels: 7.48 us -> 8.78 us  [call(): pl.pallas_call(kernel, in_specs=[SMEM] * len(scalars) + [VMEM] * len(arra...]
  transfers between devices with their start and end apart: 11 -> 11, of which waited for: 4 -> 5; matrix products, arithmetic and copies ran while one was open for 0% -> 0% of each run, Pallas kernels for 8% -> 10%
where the time goes in v4:
time: 89.2 us; the launch traced here: 88.7 us
  starting transfers between devices  52.7 us (59%)
  waiting for transfers between devices  20 us (22%)
  Pallas kernels  9.6 us (11%)
  local copies, waits for them, and re-layouts  5.31 us (6%)
    ppermute x11, starting transfers between devices, send(): return lax.ppermute(value, ('row', 'col', 'layer'), pairs)  52.7 us
    ppermute x11, waiting for transfers between devices, send(): return lax.ppermute(value, ('row', 'col', 'layer'), pairs)  20 us
    pallas_call x8, Pallas kernels, call(): pl.pallas_call(kernel, in_specs=[SMEM] * len(scalars) + [VMEM] * len(arra...  8.78 us
    unnamed x10, local copies, waits for them, and re-layouts  5.31 us
  transfers between devices with their start and end apart: 11, of which 5 were waited for; matrix products, arithmetic and copies ran while one was open for 0% of the time, Pallas kernels for 10%

profile of v4, /device:TPU:9, one launch (start us, length us, event | category | flops | bytes accessed | tf_op | source)
XLA Modules:
  0.0 88.7 jit_solution(6642543034612596713)
XLA Ops:
  0.0 0.8 pad_add_fusion.pack.pack_ref.b_lists
  0.8 0.0 copy-start
  0.8 1.2 %copy-done = bf16[1,1,1,16,2,128,128]{6,5,4,3,2,1,0:T(8,128)(2,1)S(1)} copy-done((bf16[1,1,1,16,2,128,128]{6,5,4,3,2,1,0:T(8,128)(2,1)S(1)}, bf16[1,1,1,16,2,128,128]{6,5,4,3,2,1,0:T(8,128)(2,1)}, u32[]{:S(2)}) %copy-start) | copy-done | bytes 1048600
  2.0 4.8 %collective-permute-start = (bf16[1040,128]{1,0:T(8,128)(2,1)S(1)}, bf16[1040,128]{1,0:T(8,128)(2,1)S(1)}, u32[]{:S(2)}, u32[]{:S(2)}) collective-permute-start(bf16[1040,128]{1,0:T(8,128)(2,1)S(1)} %head.1), channel_id=1, source_target_pairs={{0,62},{1,63},{2,32},{3,33},{4,34},{5,35},{6,36},{7,37},{8,38},{9,... | collective-permute-start | bytes 798728 | tf_op jit(solution)/shard_map/send_a0/ppermute | solution.py:211
  6.8 0.0 copy-start.1
  6.8 1.2 %copy-done.1 = bf16[1,1,1,16,2,128,128]{6,5,4,3,2,1,0:T(8,128)(2,1)S(1)} copy-done((bf16[1,1,1,16,2,128,128]{6,5,4,3,2,1,0:T(8,128)(2,1)S(1)}, bf16[1,1,1,16,2,128,128]{6,5,4,3,2,1,0:T(8,128)(2,1)}, u32[]{:S(2)}) %copy-start.1) | copy-done | bytes 1048600
  8.0 2.9 %step0.1 = (f32[1024,256]{1,0:T(8,128)S(1)}, s16[2064,128]{1,0:T(8,128)(2,1)S(1)}, bf16[1024,128]{1,0:T(8,128)(2,1)S(1)}, bf16[1024,128]{1,0:T(8,128)(2,1)S(1)}, bf16[1024,128]{1,0:T(8,128)(2,1)S(1)}) custom-call(s32[1]{0:T(128)} %bitcast.half, s32[8,48]{1,0:T(8,128)S(1)} %pad_add_fusion.pack.pack_ref.b_lists, bf16[4096,128]{1,0:T(8,128)(2,1)S(1)} %bitcast.20, ...), custom_call_target="tpu_custom_call" | custom-call | flops 2000000000 | tf_op jit(solution)/shard_map/step0/pallas_call | solution.py:164
  10.9 0.0 copy-start.3
  10.9 1.0 %copy-done.3 = f32[1024,256]{1,0:T(8,128)} copy-done((f32[1024,256]{1,0:T(8,128)}, f32[1024,256]{1,0:T(8,128)S(1)}, u32[]{:S(2)}) %copy-start.3) | copy-done | bytes 1048600
  11.9 2.1 %collective-permute-start.3 = (s16[2064,128]{1,0:T(8,128)(2,1)S(1)}, s16[2064,128]{1,0:T(8,128)(2,1)S(1)}, u32[]{:S(2)}, u32[]{:S(2)}) collective-permute-start(s16[2064,128]{1,0:T(8,128)(2,1)S(1)} %get-tuple-element.24), channel_id=1, source_target_pairs={{1,0},{3,2},{5,4},{7,6},{9,8},{11,10},{13,12},{15,14},{17,16},{19,... | collective-permute-start | bytes 1585160 | tf_op jit(solution)/shard_map/send_layer_down/ppermute | solution.py:211
  14.0 5.4 %collective-permute-start.1 = (s32[8,48]{1,0:T(8,128)S(1)}, s32[8,48]{1,0:T(8,128)S(1)}, u32[]{:S(2)}, u32[]{:S(2)}) collective-permute-start(s32[8,48]{1,0:T(8,128)S(1)} %pad_add_fusion.pack.pack_ref.b_lists), channel_id=1, source_target_pairs={{0,32},{1,33},{2,34},{3,35},{4,36},{5,37},{6,38},{7,39},{8,40},{9,... | collective-permute-start | bytes 4616 | tf_op jit(solution)/shard_map/send_c_cols/ppermute | solution.py:211
  19.4 11.2 %collective-permute-start.4 = (bf16[1024,128]{1,0:T(8,128)(2,1)S(1)}, bf16[1024,128]{1,0:T(8,128)(2,1)S(1)}, u32[]{:S(2)}, u32[]{:S(2)}) collective-permute-start(bf16[1024,128]{1,0:T(8,128)(2,1)S(1)} %get-tuple-element.22), channel_id=1, source_target_pairs={{0,62},{1,63},{2,32},{3,33},{4,34},{5,35},{6,36},{7,37},{8,38},{9,... | collective-permute-start | bytes 786440 | tf_op jit(solution)/shard_map/send_a1/ppermute | solution.py:211
  30.6 0.0 collective-permute-done.a_ref
  30.6 0.0 collective-permute-done.1.c_lists
  30.7 0.0 copy-start.2
  30.7 1.9 %copy-done.2 = bf16[1,1,1,48,2,128,128]{6,5,4,3,2,1,0:T(8,128)(2,1)S(1)} copy-done((bf16[1,1,1,48,2,128,128]{6,5,4,3,2,1,0:T(8,128)(2,1)S(1)}, bf16[1,1,1,48,2,128,128]{6,5,4,3,2,1,0:T(8,128)(2,1)}, u32[]{:S(2)}) %copy-start.2) | copy-done | bytes 3145752
  32.6 1.2 %step1_part0.1 = s16[1040,128]{1,0:T(8,128)(2,1)S(1)} custom-call(s32[1]{0:T(128)} %bitcast.11.first, s32[16,48]{1,0:T(8,128)S(1)} %slice_convert_fusion.a_lists, s32[8,48]{1,0:T(8,128)S(1)} %pad_add_fusion.pack.pack_ref.b_lists, s32[8,48]{1,0:T(8,128)S(1)} %collective-permute-done.1.c_lists, bf16[1040,128]{1,0:T(8,128)(2,1)S(1)} %collective-permute-done.a_ref, ...), custom_call_target="tpu_custom_call" | custom-call | flops 6000000000 | tf_op jit(solution)/shard_map/step1_part0/pallas_call | solution.py:164
  33.7 5.9 %collective-permute-start.2 = (s16[1040,128]{1,0:T(8,128)(2,1)S(1)}, s16[1040,128]{1,0:T(8,128)(2,1)S(1)}, u32[]{:S(2)}, u32[]{:S(2)}) collective-permute-start(s16[1040,128]{1,0:T(8,128)(2,1)S(1)} %step1_part0.1), channel_id=1, source_target_pairs={{0,481},{1,480},{2,483},{3,482},{4,485},{5,484},{6,487},{7,486},{8... | collective-permute-start | bytes 798728 | tf_op jit(solution)/shard_map/send_c0/ppermute | solution.py:211
  39.6 1.9 %collective-permute-start.7 = (bf16[1024,128]{1,0:T(8,128)(2,1)S(1)}, bf16[1024,128]{1,0:T(8,128)(2,1)S(1)}, u32[]{:S(2)}, u32[]{:S(2)}) collective-permute-start(bf16[1024,128]{1,0:T(8,128)(2,1)S(1)} %get-tuple-element.26), channel_id=1, source_target_pairs={{0,62},{1,63},{2,32},{3,33},{4,34},{5,35},{6,36},{7,37},{8,38},{9,... | collective-permute-start | bytes 786440 | tf_op jit(solution)/shard_map/send_a2/ppermute | solution.py:211
  41.6 0.0 collective-permute-done.4.a_ref
  41.6 0.0 collective-permute-done.3.refs_0_
  41.6 1.2 %step1_part1.1 = s16[1040,128]{1,0:T(8,128)(2,1)S(1)} custom-call(s32[1]{0:T(128)} %bitcast.12.first, s32[16,48]{1,0:T(8,128)S(1)} %slice_convert_fusion.a_lists, s32[8,48]{1,0:T(8,128)S(1)} %pad_add_fusion.pack.pack_ref.b_lists, s32[8,48]{1,0:T(8,128)S(1)} %collective-permute-done.1.c_lists, bf16[1024,128]{1,0:T(8,128)(2,1)S(1)} %collective-permute-done.4.a_ref, ...), custom_call_target="tpu_custom_call" | custom-call | flops 24999999488 | tf_op jit(solution)/shard_map/step1_part1/pallas_call | solution.py:164
  42.8 9.1 %collective-permute-start.5 = (s16[1040,128]{1,0:T(8,128)(2,1)S(1)}, s16[1040,128]{1,0:T(8,128)(2,1)S(1)}, u32[]{:S(2)}, u32[]{:S(2)}) collective-permute-start(s16[1040,128]{1,0:T(8,128)(2,1)S(1)} %step1_part1.1), channel_id=1, source_target_pairs={{0,481},{1,480},{2,483},{3,482},{4,485},{5,484},{6,487},{7,486},{8... | collective-permute-start | bytes 798728 | tf_op jit(solution)/shard_map/send_c1/ppermute | solution.py:211
  51.9 3.5 %collective-permute-start.9 = (bf16[1024,128]{1,0:T(8,128)(2,1)S(1)}, bf16[1024,128]{1,0:T(8,128)(2,1)S(1)}, u32[]{:S(2)}, u32[]{:S(2)}) collective-permute-start(bf16[1024,128]{1,0:T(8,128)(2,1)S(1)} %get-tuple-element.30), channel_id=1, source_target_pairs={{0,62},{1,63},{2,32},{3,33},{4,34},{5,35},{6,36},{7,37},{8,38},{9,... | collective-permute-start | bytes 786440 | tf_op jit(solution)/shard_map/send_a3/ppermute | solution.py:211
  55.4 0.6 collective-permute-done.7.a_ref
  56.0 1.2 %step1_part2.1 = s16[1040,128]{1,0:T(8,128)(2,1)S(1)} custom-call(s32[1]{0:T(128)} %bitcast.13.first, s32[16,48]{1,0:T(8,128)S(1)} %slice_convert_fusion.a_lists, s32[8,48]{1,0:T(8,128)S(1)} %pad_add_fusion.pack.pack_ref.b_lists, s32[8,48]{1,0:T(8,128)S(1)} %collective-permute-done.1.c_lists, bf16[1024,128]{1,0:T(8,128)(2,1)S(1)} %collective-permute-done.7.a_ref, ...), custom_call_target="tpu_custom_call" | custom-call | flops 24999999488 | tf_op jit(solution)/shard_map/step1_part2/pallas_call | solution.py:164
  57.2 5.6 %collective-permute-start.8 = (s16[1040,128]{1,0:T(8,128)(2,1)S(1)}, s16[1040,128]{1,0:T(8,128)(2,1)S(1)}, u32[]{:S(2)}, u32[]{:S(2)}) collective-permute-start(s16[1040,128]{1,0:T(8,128)(2,1)S(1)} %step1_part2.1), channel_id=1, source_target_pairs={{0,480},{1,481},{2,482},{3,483},{4,484},{5,485},{6,486},{7,487},{8... | collective-permute-start | bytes 798728 | tf_op jit(solution)/shard_map/send_c2/ppermute | solution.py:211
  62.8 1.3 %collective-permute-start.6 = (s16[2064,128]{1,0:T(8,128)(2,1)S(1)}, s16[2064,128]{1,0:T(8,128)(2,1)S(1)}, u32[]{:S(2)}, u32[]{:S(2)}) collective-permute-start(s16[2064,128]{1,0:T(8,128)(2,1)S(1)} %get-tuple-element.24), channel_id=1, source_target_pairs={{0,1},{2,3},{4,5},{6,7},{8,9},{10,11},{12,13},{14,15},{16,17},{18,... | collective-permute-start | bytes 1585160 | tf_op jit(solution)/shard_map/send_layer_up/ppermute | solution.py:211
  64.1 7.6 %collective-permute-done.9.a_ref = bf16[1024,128]{1,0:T(8,128)(2,1)S(1)} collective-permute-done((bf16[1024,128]{1,0:T(8,128)(2,1)S(1)}, bf16[1024,128]{1,0:T(8,128)(2,1)S(1)}, u32[]{:S(2)}, u32[]{:S(2)}) %collective-permute-start.9) | collective-permute-done | bytes 262176 | tf_op jit(solution)/shard_map/send_a3/ppermute | solution.py:211
  71.8 0.0 copy-start.4
  71.8 1.2 %step1_part3.1 = s16[1040,128]{1,0:T(8,128)(2,1)S(1)} custom-call(s32[1]{0:T(128)} %bitcast.14.first, s32[16,48]{1,0:T(8,128)S(1)} %slice_convert_fusion.a_lists, s32[8,48]{1,0:T(8,128)S(1)} %pad_add_fusion.pack.pack_ref.b_lists, s32[8,48]{1,0:T(8,128)S(1)} %collective-permute-done.1.c_lists, bf16[1024,128]{1,0:T(8,128)(2,1)S(1)} %collective-permute-done.9.a_ref, ...), custom_call_target="tpu_custom_call" | custom-call | flops 24999999488 | tf_op jit(solution)/shard_map/step1_part3/pallas_call | solution.py:164
  72.9 1.9 %collective-permute-start.10 = (s16[1040,128]{1,0:T(8,128)(2,1)S(1)}, s16[1040,128]{1,0:T(8,128)(2,1)S(1)}, u32[]{:S(2)}, u32[]{:S(2)}) collective-permute-start(s16[1040,128]{1,0:T(8,128)(2,1)S(1)} %step1_part3.1), channel_id=1, source_target_pairs={{0,480},{1,481},{2,482},{3,483},{4,484},{5,485},{6,486},{7,487},{8... | collective-permute-start | bytes 798728 | tf_op jit(solution)/shard_map/send_c3/ppermute | solution.py:211
  74.9 0.0 collective-permute-done.2.part_ref
  74.9 0.0 copy-done.4
  74.9 0.1 sum_part0.1.total_ref
  75.0 0.0 collective-permute-done.5.part_ref
  75.0 0.1 sum_part1.1.total_ref
  75.1 0.1 collective-permute-done.8.part_ref
  75.3 2.8 %collective-permute-done.6.layer_ref = s16[2064,128]{1,0:T(8,128)(2,1)S(1)} collective-permute-done((s16[2064,128]{1,0:T(8,128)(2,1)S(1)}, s16[2064,128]{1,0:T(8,128)(2,1)S(1)}, u32[]{:S(2)}, u32[]{:S(2)}) %collective-permute-start.6) | collective-permute-done | bytes 528416 | tf_op jit(solution)/shard_map/send_layer_up/ppermute | solution.py:211
  78.1 1.0 %sum_early.1 = (bf16[8,2,128,128]{3,2,1,0:T(8,128)(2,1)}, f32[512,256]{1,0:T(8,128)S(1)}) custom-call(s32[1]{0:T(128)} %bitcast.half, f32[1024,256]{1,0:T(8,128)S(1)} %sum_part1.1.total_ref, s16[2064,128]{1,0:T(8,128)(2,1)S(1)} %collective-permute-done.6.layer_ref, s16[1040,128]{1,0:T(8,128)(2,1)S(1)} %collective-permute-done.8.part_ref), custom_call_target="tpu_custom_call" | custom-call | flops 1000000000 | tf_op jit(solution)/shard_map/sum_early/pallas_call | solution.py:164
  79.1 8.8 %collective-permute-done.10.part_ref = s16[1040,128]{1,0:T(8,128)(2,1)S(1)} collective-permute-done((s16[1040,128]{1,0:T(8,128)(2,1)S(1)}, s16[1040,128]{1,0:T(8,128)(2,1)S(1)}, u32[]{:S(2)}, u32[]{:S(2)}) %collective-permute-start.10) | collective-permute-done | bytes 266272 | tf_op jit(solution)/shard_map/send_c3/ppermute | solution.py:211
  87.9 0.8 sum_last.1
  (2 shorter events, 0.0 us)
Async XLA Ops:
  0.8 1.2 %copy-start = (bf16[1,1,1,16,2,128,128]{6,5,4,3,2,1,0:T(8,128)(2,1)S(1)}, bf16[1,1,1,16,2,128,128]{6,5,4,3,2,1,0:T(8,128)(2,1)}, u32[]{:S(2)}) copy-start(bf16[1,1,1,16,2,128,128]{6,5,4,3,2,1,0:T(8,128)(2,1)} %param.7) | copy-start | bytes 3145732
  2.0 28.6 %collective-permute-start = (bf16[1040,128]{1,0:T(8,128)(2,1)S(1)}, bf16[1040,128]{1,0:T(8,128)(2,1)S(1)}, u32[]{:S(2)}, u32[]{:S(2)}) collective-permute-start(bf16[1040,128]{1,0:T(8,128)(2,1)S(1)} %head.1), channel_id=1, source_target_pairs={{0,62},{1,63},{2,32},{3,33},{4,34},{5,35},{6,36},{7,37},{8,38},{9,... | collective-permute-start | bytes 798728 | tf_op jit(solution)/shard_map/send_a0/ppermute | solution.py:211
  6.8 1.2 %copy-start.1 = (bf16[1,1,1,16,2,128,128]{6,5,4,3,2,1,0:T(8,128)(2,1)S(1)}, bf16[1,1,1,16,2,128,128]{6,5,4,3,2,1,0:T(8,128)(2,1)}, u32[]{:S(2)}) copy-start(bf16[1,1,1,16,2,128,128]{6,5,4,3,2,1,0:T(8,128)(2,1)} %param.7) | copy-start | bytes 3145732
  10.9 1.0 %copy-start.3 = (f32[1024,256]{1,0:T(8,128)}, f32[1024,256]{1,0:T(8,128)S(1)}, u32[]{:S(2)}) copy-start(f32[1024,256]{1,0:T(8,128)S(1)} %get-tuple-element.19.total_ref) | copy-start | bytes 3145732
  11.9 29.7 %collective-permute-start.3 = (s16[2064,128]{1,0:T(8,128)(2,1)S(1)}, s16[2064,128]{1,0:T(8,128)(2,1)S(1)}, u32[]{:S(2)}, u32[]{:S(2)}) collective-permute-start(s16[2064,128]{1,0:T(8,128)(2,1)S(1)} %get-tuple-element.24), channel_id=1, source_target_pairs={{1,0},{3,2},{5,4},{7,6},{9,8},{11,10},{13,12},{15,14},{17,16},{19,... | collective-permute-start | bytes 1585160 | tf_op jit(solution)/shard_map/send_layer_down/ppermute | solution.py:211
  14.0 16.6 %collective-permute-start.1 = (s32[8,48]{1,0:T(8,128)S(1)}, s32[8,48]{1,0:T(8,128)S(1)}, u32[]{:S(2)}, u32[]{:S(2)}) collective-permute-start(s32[8,48]{1,0:T(8,128)S(1)} %pad_add_fusion.pack.pack_ref.b_lists), channel_id=1, source_target_pairs={{0,32},{1,33},{2,34},{3,35},{4,36},{5,37},{6,38},{7,39},{8,40},{9,... | collective-permute-start | bytes 4616 | tf_op jit(solution)/shard_map/send_c_cols/ppermute | solution.py:211
  19.4 22.1 %collective-permute-start.4 = (bf16[1024,128]{1,0:T(8,128)(2,1)S(1)}, bf16[1024,128]{1,0:T(8,128)(2,1)S(1)}, u32[]{:S(2)}, u32[]{:S(2)}) collective-permute-start(bf16[1024,128]{1,0:T(8,128)(2,1)S(1)} %get-tuple-element.22), channel_id=1, source_target_pairs={{0,62},{1,63},{2,32},{3,33},{4,34},{5,35},{6,36},{7,37},{8,38},{9,... | collective-permute-start | bytes 786440 | tf_op jit(solution)/shard_map/send_a1/ppermute | solution.py:211
  30.7 1.9 %copy-start.2 = (bf16[1,1,1,48,2,128,128]{6,5,4,3,2,1,0:T(8,128)(2,1)S(1)}, bf16[1,1,1,48,2,128,128]{6,5,4,3,2,1,0:T(8,128)(2,1)}, u32[]{:S(2)}) copy-start(bf16[1,1,1,48,2,128,128]{6,5,4,3,2,1,0:T(8,128)(2,1)} %param.10) | copy-start | bytes 9437188
  33.7 41.1 %collective-permute-start.2 = (s16[1040,128]{1,0:T(8,128)(2,1)S(1)}, s16[1040,128]{1,0:T(8,128)(2,1)S(1)}, u32[]{:S(2)}, u32[]{:S(2)}) collective-permute-start(s16[1040,128]{1,0:T(8,128)(2,1)S(1)} %step1_part0.1), channel_id=1, source_target_pairs={{0,481},{1,480},{2,483},{3,482},{4,485},{5,484},{6,487},{7,486},{8... | collective-permute-start | bytes 798728 | tf_op jit(solution)/shard_map/send_c0/ppermute | solution.py:211
  39.6 16.4 %collective-permute-start.7 = (bf16[1024,128]{1,0:T(8,128)(2,1)S(1)}, bf16[1024,128]{1,0:T(8,128)(2,1)S(1)}, u32[]{:S(2)}, u32[]{:S(2)}) collective-permute-start(bf16[1024,128]{1,0:T(8,128)(2,1)S(1)} %get-tuple-element.26), channel_id=1, source_target_pairs={{0,62},{1,63},{2,32},{3,33},{4,34},{5,35},{6,36},{7,37},{8,38},{9,... | collective-permute-start | bytes 786440 | tf_op jit(solution)/shard_map/send_a2/ppermute | solution.py:211
  42.8 32.2 %collective-permute-start.5 = (s16[1040,128]{1,0:T(8,128)(2,1)S(1)}, s16[1040,128]{1,0:T(8,128)(2,1)S(1)}, u32[]{:S(2)}, u32[]{:S(2)}) collective-permute-start(s16[1040,128]{1,0:T(8,128)(2,1)S(1)} %step1_part1.1), channel_id=1, source_target_pairs={{0,481},{1,480},{2,483},{3,482},{4,485},{5,484},{6,487},{7,486},{8... | collective-permute-start | bytes 798728 | tf_op jit(solution)/shard_map/send_c1/ppermute | solution.py:211
  51.9 19.9 %collective-permute-start.9 = (bf16[1024,128]{1,0:T(8,128)(2,1)S(1)}, bf16[1024,128]{1,0:T(8,128)(2,1)S(1)}, u32[]{:S(2)}, u32[]{:S(2)}) collective-permute-start(bf16[1024,128]{1,0:T(8,128)(2,1)S(1)} %get-tuple-element.30), channel_id=1, source_target_pairs={{0,62},{1,63},{2,32},{3,33},{4,34},{5,35},{6,36},{7,37},{8,38},{9,... | collective-permute-start | bytes 786440 | tf_op jit(solution)/shard_map/send_a3/ppermute | solution.py:211
  57.2 18.1 %collective-permute-start.8 = (s16[1040,128]{1,0:T(8,128)(2,1)S(1)}, s16[1040,128]{1,0:T(8,128)(2,1)S(1)}, u32[]{:S(2)}, u32[]{:S(2)}) collective-permute-start(s16[1040,128]{1,0:T(8,128)(2,1)S(1)} %step1_part2.1), channel_id=1, source_target_pairs={{0,480},{1,481},{2,482},{3,483},{4,484},{5,485},{6,486},{7,487},{8... | collective-permute-start | bytes 798728 | tf_op jit(solution)/shard_map/send_c2/ppermute | solution.py:211
  62.8 15.3 %collective-permute-start.6 = (s16[2064,128]{1,0:T(8,128)(2,1)S(1)}, s16[2064,128]{1,0:T(8,128)(2,1)S(1)}, u32[]{:S(2)}, u32[]{:S(2)}) collective-permute-start(s16[2064,128]{1,0:T(8,128)(2,1)S(1)} %get-tuple-element.24), channel_id=1, source_target_pairs={{0,1},{2,3},{4,5},{6,7},{8,9},{10,11},{12,13},{14,15},{16,17},{18,... | collective-permute-start | bytes 1585160 | tf_op jit(solution)/shard_map/send_layer_up/ppermute | solution.py:211
  71.8 3.1 %copy-start.4 = (f32[1024,256]{1,0:T(8,128)S(1)}, f32[1024,256]{1,0:T(8,128)}, u32[]{:S(2)}) copy-start(f32[1024,256]{1,0:T(8,128)} %copy-done.3) | copy-start | bytes 3145732
  72.9 15.0 %collective-permute-start.10 = (s16[1040,128]{1,0:T(8,128)(2,1)S(1)}, s16[1040,128]{1,0:T(8,128)(2,1)S(1)}, u32[]{:S(2)}, u32[]{:S(2)}) collective-permute-start(s16[1040,128]{1,0:T(8,128)(2,1)S(1)} %step1_part3.1), channel_id=1, source_target_pairs={{0,480},{1,481},{2,482},{3,483},{4,484},{5,485},{6,486},{7,487},{8... | collective-permute-start | bytes 798728 | tf_op jit(solution)/shard_map/send_c3/ppermute | solution.py:211
